TPU v7x, 512 devices: a whole 4x8x8 slice. The times are simulated.
512 devices in a mesh: row: 32 (over z, x), col: 16 (over y, core).
Axes of the slice: x: 4, y: 8, z: 8, core: 2. Of those that a mesh axis runs over, the one named last changes fastest.
Arguments:
- motion: bfloat16 [32768, 512], P(('row', 'col')), may hold values from -8 to 8
- text: bfloat16 [32768, 512], P(('row', 'col')), may hold values from -8 to 8
- pair_text: int32 [32768], P(('row', 'col')), may hold values from 0 to 32767, each once
Outputs:
- motion_grad: bfloat16 [32768, 512], P(('row', 'col'))
- text_grad: bfloat16 [32768, 512], P(('row', 'col'))
Inputs may be any that keep to these rules, and one draw needn't show every extreme that they name: `pair_text`: every text row is the positive of exactly one motion row.
All inputs are finite; a program needn't handle non-finite values.
Results may differ from a plain program's by a relative error of at most 0.022.
Values may be sent and summed in bfloat16 or wider, within the bound.
No kernel may reach another device: no remote copies, remote signals or barrier semaphores. Data moves between devices by JAX's collectives and lax.ppermute only.
A program may use at most 64 MiB of HBM per device.

v0:
```python
import jax
import jax.numpy as jnp
from jax import lax
from jax.sharding import PartitionSpec as P

TAU = 0.1


def tile_scores(rows, cols):
    return (
        lax.dot_general(rows, cols, (((1,), (1,)), ((), ())), preferred_element_type=jnp.float32)
        / TAU
    )


def per_device(motion, text, pair_text):
    pair_dev = motion.shape[0]
    n_row = lax.axis_size("row")
    n_col = lax.axis_size("col")
    width = pair_dev * n_row
    block_rows = lax.all_gather(motion, "col", axis=0, tiled=True)
    pair_rows = lax.all_gather(pair_text, "col", axis=0, tiled=True)
    block_text = lax.all_gather(text, "row", axis=0, tiled=True)
    scores = tile_scores(block_rows, block_text)
    row_peak = lax.pmax(jnp.max(scores, axis=1), "col")
    col_peak = lax.pmax(jnp.max(scores, axis=0), "row")
    row_total = lax.psum(jnp.sum(jnp.exp(scores - row_peak[:, None]), axis=1), "col")
    col_total = lax.psum(jnp.sum(jnp.exp(scores - col_peak[None, :]), axis=0), "row")
    row_lse = row_peak + jnp.log(row_total)
    col_lse = col_peak + jnp.log(col_total)
    within = lax.broadcasted_iota(jnp.int32, (1, width), 1)
    col_ids = (within // pair_dev * n_col + lax.axis_index("col")) * pair_dev + within % pair_dev
    positive = (pair_rows[:, None] == col_ids).astype(jnp.float32)
    weights = (
        (jnp.exp(scores - row_lse[:, None]) + jnp.exp(scores - col_lse[None, :]) - 2.0 * positive)
        / (2.0 * TAU)
    ).astype(jnp.bfloat16)
    part = weights
    text_grad = lax.psum_scatter(
        lax.dot_general(
            part, block_rows, (((0,), (0,)), ((), ())), preferred_element_type=jnp.float32
        ).astype(jnp.bfloat16),
        "row",
        scatter_dimension=0,
        tiled=True,
    )
    part = weights
    motion_grad = lax.psum_scatter(
        jnp.dot(part, block_text, preferred_element_type=jnp.float32).astype(jnp.bfloat16),
        "col",
        scatter_dimension=0,
        tiled=True,
    )
    return (motion_grad, text_grad)


def solution(mesh):
    return jax.shard_map(
        per_device,
        mesh=mesh,
        in_specs=(P(("row", "col"), None), P(("row", "col"), None), P(("row", "col"))),
        out_specs=(P(("row", "col"), None), P(("row", "col"), None)),
        check_vma=False,
    )
```

profile of v0, /device:TPU:1, one launch (start us, length us, event | category | flops | bytes accessed | tf_op | source)
XLA Modules:
  0.0 648.6 jit_solution(2842138059004177200)
XLA Ops:
  7.2 0.0 all-gather.3.cloned.1.call-start
  7.2 0.7 all-gather.3.cloned.1.call-update
  7.9 0.0 all-gather.5.cloned.1.call-start
  7.9 0.7 all-gather.5.cloned.1.call-update
  8.6 0.0 reduce-scatter.3.cloned.1.call-start
  8.7 1.3 dynamic-slice
  10.6 0.9 dynamic-update-slice
  11.5 12.3 %all-reduce = s32[1024]{0:T(1024)S(1)} all-reduce(s32[1024]{0:T(1024)S(1)} %dynamic-update-slice), channel_id=1, replica_groups=mesh['row'=32,'col'=16] {'col'}, use_global_device_ids=true, to_apply=%add | all-reduce | flops 1024 | bytes 8192
  23.8 33.0 %all-gather.3.cloned.1.call-done = bf16[1024,512]{1,0:T(8,128)(2,1)} async-done(((bf16[64,512]{1,0:T(8,128)(2,1)}), bf16[1024,512]{1,0:T(8,128)(2,1)}) %all-gather.3.cloned.1.call-update) | async-done | bytes 1048592 | tf_op jit(solution)/shard_map/all_gather | solution.py:21
  56.9 81.9 %all-gather.5.cloned.1.call-done = bf16[2048,512]{1,0:T(8,128)(2,1)} async-done(((bf16[64,512]{1,0:T(8,128)(2,1)}), bf16[2048,512]{1,0:T(8,128)(2,1)}) %all-gather.5.cloned.1.call-update) | async-done | bytes 2097168 | tf_op jit(solution)/shard_map/all_gather | solution.py:23
  138.7 7.5 %multiply_reduce_fusion.1 = (f32[1024]{0:T(1024)S(1)}, f32[1024,2048]{1,0:T(8,128)}) fusion(bf16[1024,512]{1,0:T(8,128)(2,1)} %all-gather.3.cloned.1.call-done, bf16[2048,512]{1,0:T(8,128)(2,1)} %all-gather.5.cloned.1.call-done), kind=kOutput, calls=%fused_computation.4 | convolution fusion | flops 2151676928 | bytes 11538432 | tf_op jit(solution)/shard_map/dot_general | solution.py:11
  146.2 27.6 %pmax.14 = f32[1024]{0:T(1024)S(1)} all-reduce(f32[1024]{0:T(1024)S(1)} %get-tuple-element.4), channel_id=1, replica_groups=mesh['row'=32,'col'=16] {'col'}, use_global_device_ids=true, to_apply=%region_1.0 | all-reduce | flops 1024 | bytes 8192 | tf_op jit(solution)/shard_map/pmax | solution.py:25
  173.8 4.6 exponential_reduce_fusion.1
  178.4 23.6 %psum.14 = f32[1024]{0:T(1024)S(1)} all-reduce(f32[1024]{0:T(1024)S(1)} %get-tuple-element.2), channel_id=1, replica_groups=mesh['row'=32,'col'=16] {'col'}, use_global_device_ids=true, to_apply=%region_3.0 | all-reduce | flops 1024 | bytes 8192 | tf_op jit(solution)/shard_map/psum | solution.py:27
  201.9 59.0 %pmax.15 = f32[2048]{0:T(1024)S(1)} all-reduce(f32[2048]{0:T(1024)S(1)} %get-tuple-element.3), channel_id=1, replica_groups=mesh['row'=32,'col'=16] {'row'}, use_global_device_ids=true, to_apply=%region_5.0 | all-reduce | flops 2048 | bytes 16384 | tf_op jit(solution)/shard_map/pmax | solution.py:26
  260.9 4.8 exponential_reduce_fusion
  265.7 0.0 copy-start.1
  265.7 56.9 %psum.15 = f32[2048]{0:T(1024)S(1)} all-reduce(f32[2048]{0:T(1024)S(1)} %exponential_reduce_fusion), channel_id=1, replica_groups=mesh['row'=32,'col'=16] {'row'}, use_global_device_ids=true, to_apply=%region_7.0 | all-reduce | flops 2048 | bytes 16384 | tf_op jit(solution)/shard_map/psum | solution.py:28
  322.6 6.4 multiply_convert_fusion
  329.0 0.0 copy-start
  329.0 1.9 copy-done
  330.9 0.0 copy-done.1
  330.9 0.0 copy-start.2
  330.9 3.3 convolution_convert_fusion.1
  334.3 0.0 reduce-scatter.3.cloned.1.call-update
  334.3 0.0 reduce-scatter.5.cloned.1.call-start
  334.3 0.0 copy-done.2
  334.4 5.9 convolution_convert_fusion
  340.3 0.0 reduce-scatter.5.cloned.1.call-update
  340.3 78.2 %reduce-scatter.3.cloned.1.call-done = bf16[64,512]{1,0:T(8,128)(2,1)} async-done(((bf16[1024,512]{1,0:T(8,128)(2,1)}), bf16[64,512]{1,0:T(8,128)(2,1)}) %reduce-scatter.3.cloned.1.call-update) | async-done | bytes 65552 | tf_op jit(solution)/shard_map/reduce_scatter | solution.py:48
  418.5 223.6 %reduce-scatter.5.cloned.1.call-done = bf16[64,512]{1,0:T(8,128)(2,1)} async-done(((bf16[2048,512]{1,0:T(8,128)(2,1)}), bf16[64,512]{1,0:T(8,128)(2,1)}) %reduce-scatter.5.cloned.1.call-update) | async-done | bytes 65552 | tf_op jit(solution)/shard_map/reduce_scatter | solution.py:39
  (4 shorter events, 0.0 us)
Async XLA Ops:
  7.2 49.7 %all-gather.3.cloned.1.call-start = ((), (), s32[]{:S(2)}) async-start(), calls=%async_computation.2 | async-start | bytes 1114112 | tf_op jit(solution)/shard_map/all_gather | solution.py:21
  7.9 130.8 %all-gather.5.cloned.1.call-start = ((), (), s32[]{:S(2)}) async-start(), calls=%async_computation.3 | async-start | bytes 2162688 | tf_op jit(solution)/shard_map/all_gather | solution.py:23
  8.6 409.8 %reduce-scatter.3.cloned.1.call-start = ((), (), s32[]{:S(2)}) async-start(), calls=%async_computation.4 | async-start | bytes 1114112 | tf_op jit(solution)/shard_map/reduce_scatter | solution.py:48
  265.7 65.3 %copy-start.1 = (bf16[2048,512]{1,0:T(8,128)(2,1)S(1)}, bf16[2048,512]{1,0:T(8,128)(2,1)}, u32[]{:S(2)}) copy-start(bf16[2048,512]{1,0:T(8,128)(2,1)} %all-gather.5.cloned.1.call-done) | copy-start | bytes 6291460
  329.0 1.9 copy-start
  330.9 3.4 copy-start.2
  334.3 307.8 %reduce-scatter.5.cloned.1.call-start = ((), (), s32[]{:S(2)}) async-start(), calls=%async_computation.5 | async-start | bytes 2162688 | tf_op jit(solution)/shard_map/reduce_scatter | solution.py:39
Sparse Core Ops, SparseCore 0:
  10.1 46.6 all-gather.2
  60.0 78.6 all-gather.4
  334.4 83.9 reduce-scatter.2
  423.9 218.1 reduce-scatter.4
where the time goes:
time: 653 us; the launch traced here: 649 us
  waiting for transfers between devices  418 us (64%)
  blocking collectives  179 us (27%)
  matrix products  16.7 us (3%)
  other arithmetic  15.8 us (2%)
  between operations  14.5 us (2%)
    reduce_scatter x1, waiting for transfers between devices, per_device(): lax.psum_scatter(lax.dot_general(part, block_rows, (((0,), (0,)), ((), ()...  224 us
    all_gather x1, waiting for transfers between devices, per_device(): block_text = lax.all_gather(text, 'row', axis=0, tiled=True)  81.9 us
    reduce_scatter x1, waiting for transfers between devices, per_device(): lax.psum_scatter(jnp.dot(part, block_text, preferred_element_type=jnp.flo...  78.2 us
    pmax x1, blocking collectives, per_device(): col_peak = lax.pmax(jnp.max(scores, axis=0), 'row')  59 us
    psum x1, blocking collectives, per_device(): lax.psum(jnp.sum(jnp.exp(scores - col_peak[None, :]), axis=0), 'row')  56.9 us
    all_gather x1, waiting for transfers between devices, per_device(): block_rows = lax.all_gather(motion, 'col', axis=0, tiled=True)  33 us
    pmax x1, blocking collectives, per_device(): row_peak = lax.pmax(jnp.max(scores, axis=1), 'col')  27.6 us
    psum x1, blocking collectives, per_device(): lax.psum(jnp.sum(jnp.exp(scores - row_peak[:, None]), axis=1), 'col')  23.6 us
  transfers between devices with their start and end apart: 4, of which 4 were waited for; matrix products, arithmetic and copies ran while one was open for 1% of the time, Pallas kernels for 0%

commit v1 on v0

v1 whole, which is shorter than its diff:
```python
import jax
import jax.numpy as jnp
from jax import lax
from jax.sharding import Mesh, PartitionSpec as P

TAU = 0.1
AX = "d"
NZ, NX, NY, NC = 8, 4, 8, 2
DEVICES = NZ * NX * NY * NC


def dev(z, x, y, c):
    return ((z * NX + x) * NY + y) * NC + c


MOTION_PAIRS = ((0, 1), (2, 3))
TEXT_PAIRS = ((0, 3), (1, 2))
MOTION_GROUPS = [
    [dev(z, x, y, 1) for x in pair for y in range(NY)] for z in range(NZ) for pair in MOTION_PAIRS
]
TEXT_GROUPS = [
    [dev(z, x, y, 0) for x in pair for z in range(NZ)] for y in range(NY) for pair in TEXT_PAIRS
]
GROUPS = MOTION_GROUPS + TEXT_GROUPS
SWAP = [(i, i ^ 1) for i in range(DEVICES)]
TO_TEXT = [(i, i ^ 1) for i in range(1, DEVICES, 2)]
TO_MOTION = [(i, i ^ 1) for i in range(0, DEVICES, 2)]
G = 16


def swap(x):
    return lax.ppermute(x, AX, SWAP)


def exchange(x):
    return lax.all_to_all(x, AX, 0, 0, axis_index_groups=GROUPS)


def lse(x, axis):
    peak = jnp.max(x, axis=axis, keepdims=True)
    return jnp.squeeze(peak, axis) + jnp.log(jnp.sum(jnp.exp(x - peak), axis=axis))


def text_ids(d):
    chip = d // NC
    y = chip % NY
    x = chip // NY % NX
    n = lax.broadcasted_iota(jnp.int32, (1, G * 128), 1)
    k, rest = n // 128, n % 128
    outer = (x == 1) | (x == 2)
    xs = jnp.where(k < NZ, jnp.where(outer, 1, 0), jnp.where(outer, 2, 3))
    return (((k % NZ) * NX + xs) * NY + y) * 128 + rest


def per_device(motion, text, pair_text):
    n = motion.shape[0]
    d = lax.axis_index(AX)
    core = d % NC
    is_text = core == 0
    got = swap(jnp.where(is_text, motion, text))
    mine = jnp.where(is_text, jnp.concatenate([text, got]), jnp.concatenate([got, motion]))
    block = exchange(jnp.broadcast_to(mine[None], (G, 2 * n, mine.shape[1]))).reshape(G * 2 * n, -1)
    pair_got = swap(pair_text)
    other = swap(block)
    cols = jnp.where(is_text, block, other)
    rows = jnp.where(is_text, other[: G * n], block[G * n :])
    scores = (
        lax.dot_general(rows, cols, (((1,), (1,)), ((), ())), preferred_element_type=jnp.float32)
        / TAU
    )
    row_part = lse(scores, 1)
    col_part = lse(scores, 0)
    pad = jnp.zeros_like(row_part)
    stat_got = swap(jnp.where(is_text, jnp.concatenate([row_part, pad]), col_part))
    stat = jnp.where(
        is_text,
        jnp.logaddexp(col_part, stat_got),
        jnp.concatenate([stat_got[: G * n], row_part]),
    )
    pairs = jnp.concatenate([pair_got, pair_text]).astype(jnp.float32)
    stats = exchange(
        jnp.broadcast_to(jnp.concatenate([stat, pairs]).reshape(1, 17, 128), (G, 17, 128))
    )
    total = lse(stats[:, :16].reshape(G, 2048), 0)
    pair_all = stats[:, 16].reshape(2048)
    sent = jnp.where(is_text, total, jnp.concatenate([total[:1024], pair_all[:1024]]))
    total_got = swap(sent)
    col_lse = jnp.where(is_text, total, total_got)
    row_lse = jnp.where(is_text, total_got[:1024], total[1024:])
    pair_rows = jnp.where(is_text, total_got[1024:], pair_all[1024:]).astype(jnp.int32)
    positive = (pair_rows[:, None] == text_ids(d)).astype(jnp.float32)
    weights = (
        (jnp.exp(scores - row_lse[:, None]) + jnp.exp(scores - col_lse[None, :]) - 2.0 * positive)
        / (2.0 * TAU)
    ).astype(jnp.bfloat16)
    text_part = lax.dot_general(
        weights, rows, (((0,), (0,)), ((), ())), preferred_element_type=jnp.float32
    )
    motion_part = jnp.dot(weights, cols, preferred_element_type=jnp.float32).astype(jnp.bfloat16)
    text_got = lax.ppermute(text_part.astype(jnp.bfloat16), AX, TO_TEXT)
    motion_got = lax.ppermute(motion_part, AX, TO_MOTION)
    part = jnp.where(
        is_text,
        (text_part + text_got.astype(jnp.float32)).astype(jnp.bfloat16),
        jnp.concatenate([motion_got, motion_part]),
    )
    grads = exchange(part.reshape(G, 2 * n, -1))
    grad = jnp.sum(grads.astype(jnp.float32), axis=0).astype(jnp.bfloat16)
    grad_got = swap(jnp.where(is_text, grad[n:], grad[:n]))
    motion_grad = jnp.where(is_text, grad_got, grad[n:])
    text_grad = jnp.where(is_text, grad[:n], grad_got)
    return (motion_grad, text_grad)


def solution(mesh):
    flat = Mesh(mesh.devices.reshape(DEVICES), (AX,))
    return jax.shard_map(
        per_device,
        mesh=flat,
        in_specs=(P(AX, None), P(AX, None), P(AX)),
        out_specs=(P(AX, None), P(AX, None)),
        check_vma=False,
    )
```

time: 653 us -> 142 us (0.22)
  waiting for transfers between devices: 418 us -> 15.8 us
  blocking collectives: 179 us -> 63.8 us
  starting transfers between devices: 0.16 us -> 37.1 us
  between operations: 14.5 us -> 0.99 us
  matrix products: 16.7 us -> 7.21 us
    reduce_scatter x2 -> x0, waiting for transfers between devices: 302 us -> none  [the longest x1 224 us: per_device(): lax.psum_scatter(lax.dot_general(part, block_rows, (((0,), (0,)), ((), ()...]
    all_gather x2 -> x0, waiting for transfers between devices: 115 us -> none  [the longest x1 81.9 us: per_device(): block_text = lax.all_gather(text, 'row', axis=0, tiled=True)]
    pmax x2 -> x0, blocking collectives: 86.5 us -> none  [the longest x1 59 us: per_device(): col_peak = lax.pmax(jnp.max(scores, axis=0), 'row')]
    psum x2 -> x0, blocking collectives: 80.5 us -> none  [the longest x1 56.9 us: per_device(): lax.psum(jnp.sum(jnp.exp(scores - col_peak[None, :]), axis=0), 'row')]
    all_to_all x0 -> x2, blocking collectives: none -> 63.8 us  [exchange(): return lax.all_to_all(x, AX, 0, 0, axis_index_groups=GROUPS)]
    ppermute x0 -> x8, starting transfers between devices: none -> 30.2 us  [the longest x6 26.3 us: swap(): return lax.ppermute(x, AX, SWAP)]
    unnamed x1 -> x0, blocking collectives: 12.3 us -> none
    dot_general x3, matrix products: 16.7 us -> 7.21 us  [the longest x1 2.46 us: per_device(): lax.dot_general(weights, rows, (((0,), (0,)), ((), ())), preferred_elemen...]
  transfers between devices with their start and end apart: 4 -> 9, of which waited for: 4 -> 7; matrix products, arithmetic and copies ran while one was open for 1% -> 6% of each run, Pallas kernels for 0% -> 0%
where the time goes in v1:
time: 142 us
  blocking collectives  63.8 us (45%)
  starting transfers between devices  37.1 us (26%)
  waiting for transfers between devices  15.8 us (11%)
  other arithmetic  14.6 us (10%)
  matrix products  7.21 us (5%)
  local copies, waits for them, and re-layouts  2 us (1%)
    all_to_all x2, blocking collectives, exchange(): return lax.all_to_all(x, AX, 0, 0, axis_index_groups=GROUPS)  63.8 us
    ppermute x6, starting transfers between devices, swap(): return lax.ppermute(x, AX, SWAP)  26.3 us
    all_to_all x1, waiting for transfers between devices, exchange(): return lax.all_to_all(x, AX, 0, 0, axis_index_groups=GROUPS)  7.55 us
    all_to_all x1, starting transfers between devices, exchange(): return lax.all_to_all(x, AX, 0, 0, axis_index_groups=GROUPS)  6.93 us
    convert_element_type x1, other arithmetic, per_device(): weights = ((jnp.exp(scores - row_lse[:, None]) + jnp.exp(scores - col_lse...  6.4 us
    ppermute x6, waiting for transfers between devices, swap(): return lax.ppermute(x, AX, SWAP)  5.02 us
    reduce_sum x3, other arithmetic, lse(): jnp.sum(jnp.exp(x - peak), axis=axis)  4.13 us
    ppermute x1, waiting for transfers between devices, per_device(): motion_got = lax.ppermute(motion_part, AX, TO_MOTION)  3.25 us
  transfers between devices with their start and end apart: 9, of which 7 were waited for; matrix products, arithmetic and copies ran while one was open for 6% of the time, Pallas kernels for 0%

profile of v1, /device:TPU:1, one launch (start us, length us, event | category | flops | bytes accessed | tf_op | source)
XLA Modules:
  0.0 141.5 jit_solution(12779621861165287798)
XLA Ops:
  0.6 0.0 copy-start.3
  0.7 0.9 broadcast_select_fusion.6
  1.5 8.8 %collective-permute-start = (bf16[64,512]{1,0:T(8,128)(2,1)S(1)}, bf16[64,512]{1,0:T(8,128)(2,1)S(1)}, u32[]{:S(2)}, u32[]{:S(2)}) collective-permute-start(bf16[64,512]{1,0:T(8,128)(2,1)S(1)} %broadcast_select_fusion.6), channel_id=1, source_target_pairs={{0,1},{1,0},{2,3},{3,2},{4,5},{5,4},{6,7},{7,6},{8,9},{9,8},{10,11... | collective-permute-start | bytes 196616 | tf_op jit(solution)/shard_map/ppermute | solution.py:32
  10.3 0.9 collective-permute-done
  11.2 0.9 maximum_select_fusion
  12.1 0.2 broadcast_in_dim.12
  12.3 30.0 %all_to_all.15 = bf16[16,128,512]{2,1,0:T(8,128)(2,1)S(1)} all-to-all(bf16[16,128,512]{2,1,0:T(8,128)(2,1)S(1)} %broadcast_in_dim.12), channel_id=1, replica_groups={{1,3,5,7,9,11,13,15,17,19,21,23,25,27,29,31},{33,35,37,39,41,43,45,47,4..., dimensions={0} | all-to-all | bytes 4194304 | tf_op jit(solution)/shard_map/all_to_all | solution.py:36
  42.3 8.8 %collective-permute-start.1 = (bf16[2048,512]{1,0:T(8,128)(2,1)S(1)}, bf16[2048,512]{1,0:T(8,128)(2,1)S(1)}, u32[]{:S(2)}, u32[]{:S(2)}) collective-permute-start(bf16[2048,512]{1,0:T(8,128)(2,1)S(1)} %bitcast.22), channel_id=1, source_target_pairs={{0,1},{1,0},{2,3},{3,2},{4,5},{5,4},{6,7},{7,6},{8,9},{9,8},{10,11... | collective-permute-start | bytes 6291464 | tf_op jit(solution)/shard_map/ppermute | solution.py:32
  51.1 0.0 copy-done.3
  51.1 1.9 %collective-permute-start.3 = (s32[64]{0:T(128)S(1)}, s32[64]{0:T(128)S(1)}, u32[]{:S(2)}, u32[]{:S(2)}) collective-permute-start(s32[64]{0:T(128)S(1)} %copy-done.3), channel_id=1, source_target_pairs={{0,1},{1,0},{2,3},{3,2},{4,5},{5,4},{6,7},{7,6},{8,9},{9,8},{10,11... | collective-permute-start | bytes 776 | tf_op jit(solution)/shard_map/ppermute | solution.py:32
  53.0 0.1 slice.74
  53.1 1.7 %collective-permute-done.1 = bf16[2048,512]{1,0:T(8,128)(2,1)S(1)} collective-permute-done((bf16[2048,512]{1,0:T(8,128)(2,1)S(1)}, bf16[2048,512]{1,0:T(8,128)(2,1)S(1)}, u32[]{:S(2)}, u32[]{:S(2)}) %collective-permute-start.1) | collective-permute-done | bytes 2097184 | tf_op jit(solution)/shard_map/ppermute | solution.py:32
  54.8 0.0 copy-start.1
  54.8 0.2 slice_select_fusion
  55.0 2.4 %multiply_reduce_fusion.1 = (f32[2048]{0:T(1024)S(1)}, f32[1024,2048]{1,0:T(8,128)S(1)}) fusion(bf16[1024,512]{1,0:T(8,128)(2,1)S(1)} %slice_select_fusion, bf16[2048,512]{1,0:T(8,128)(2,1)S(1)} %bitcast.23, bf16[2048,512]{1,0:T(8,128)(2,1)S(1)} %collective-permute-done.1, pred[]{:T(512)S(6)} %eq.29), kind=kOutput, calls=%fused_computation.4 | convolution fusion | flops 2152724480 | bytes 13639681 | tf_op jit(solution)/shard_map/dot_general | solution.py:68
  57.4 0.0 copy-done.1
  57.4 0.0 copy-start
  57.4 2.2 %exponential_reduce_fusion.1 = (f32[2048]{0:T(1024)S(1)}, f32[1024]{0:T(1024)S(1)}) fusion(f32[1024,2048]{1,0:T(8,128)S(1)} %get-tuple-element.11, f32[2048]{0:T(1024)S(1)} %get-tuple-element.10), kind=kLoop, calls=%fused_computation.2 | loop fusion | flops 8385536 | bytes 8409088 | tf_op jit(solution)/shard_map/reduce_sum | solution.py:41
  59.6 1.0 copy-done
  60.6 1.9 %exponential_reduce_fusion = f32[1024]{0:T(1024)S(1)} fusion(f32[1024,2048]{1,0:T(8,128)S(1)} %get-tuple-element.11, f32[1024]{0:T(1024)S(1)} %get-tuple-element.3), kind=kLoop, calls=%fused_computation.1 | loop fusion | flops 6290432 | bytes 8396800 | tf_op jit(solution)/shard_map/reduce_sum | solution.py:41
  62.6 2.3 %collective-permute-start.2 = (f32[2048]{0:T(1024)S(1)}, f32[2048]{0:T(1024)S(1)}, u32[]{:S(2)}, u32[]{:S(2)}) collective-permute-start(f32[2048]{0:T(1024)S(1)} %pad_select_fusion), channel_id=1, source_target_pairs={{0,1},{1,0},{2,3},{3,2},{4,5},{5,4},{6,7},{7,6},{8,9},{9,8},{10,11... | collective-permute-start | bytes 24584 | tf_op jit(solution)/shard_map/ppermute | solution.py:32
  64.9 0.0 collective-permute-done.3
  64.9 0.1 add_convert_fusion.1
  65.0 0.7 collective-permute-done.2
  65.7 0.7 broadcast_in_dim.16
  66.4 6.9 %all-to-all-start.1 = ((f32[16,17,128]{2,1,0:T(8,128)}), f32[16,17,128]{2,1,0:T(8,128)S(1)}, u32[]{:S(2)}, u32[]{:S(2)}) async-start(f32[16,17,128]{2,1,0:T(8,128)} %broadcast_in_dim.16), calls=%async_computation.1 | async-start | bytes 393216 | tf_op jit(solution)/shard_map/all_to_all | solution.py:36
  73.4 7.6 %all-to-all-done.1 = f32[16,17,128]{2,1,0:T(8,128)S(1)} async-done(((f32[16,17,128]{2,1,0:T(8,128)}), f32[16,17,128]{2,1,0:T(8,128)S(1)}, u32[]{:S(2)}, u32[]{:S(2)}) %all-to-all-start.1) | async-done | bytes 139296 | tf_op jit(solution)/shard_map/all_to_all | solution.py:36
  81.1 2.3 %collective-permute-start.4 = (f32[2048]{0:T(1024)S(1)}, f32[2048]{0:T(1024)S(1)}, u32[]{:S(2)}, u32[]{:S(2)}) collective-permute-start(f32[2048]{0:T(1024)S(1)} %maximum_select_fusion.2), channel_id=1, source_target_pairs={{0,1},{1,0},{2,3},{3,2},{4,5},{5,4},{6,7},{7,6},{8,9},{9,8},{10,11... | collective-permute-start | bytes 24584 | tf_op jit(solution)/shard_map/ppermute | solution.py:32
  83.4 0.8 collective-permute-done.4
  84.2 6.4 %multiply_convert_fusion = bf16[1024,2048]{1,0:T(8,128)(2,1)S(1)} fusion(f32[1024,2048]{1,0:T(8,128)} %copy-done, s32[2048]{0:T(1024)S(1)} %fusion.14, f32[2048]{0:T(1024)S(1)} %bitcast_select_fusion, f32[1024]{0:T(1024)S(1)} %get-tuple-element.9, s32[1024]{0:T(1024)S(1)} %get-tuple-element.8), kind=kLoop, calls=%fused_computation | loop fusion | flops 18874368 | bytes 12607488 | tf_op jit(solution)/shard_map/convert_element_type | solution.py:95
  90.6 0.0 copy-start.2
  90.6 2.5 %fusion.20 = (bf16[2048,512]{1,0:T(8,128)(2,1)S(1)}, f32[2048,512]{1,0:T(8,128)S(1)}) fusion(bf16[1024,2048]{1,0:T(8,128)(2,1)S(1)} %multiply_convert_fusion, bf16[1024,512]{1,0:T(8,128)(2,1)S(1)} %slice_select_fusion), kind=kOutput, calls=%fused_computation.55 | convolution fusion | flops 2148532224 | bytes 11534336 | tf_op jit(solution)/shard_map/dot_general | solution.py:96
  93.1 2.6 %collective-permute-start.5 = (bf16[2048,512]{1,0:T(8,128)(2,1)S(1)}, bf16[2048,512]{1,0:T(8,128)(2,1)S(1)}, u32[]{:S(2)}, u32[]{:S(2)}) collective-permute-start(bf16[2048,512]{1,0:T(8,128)(2,1)S(1)} %get-tuple-element.12), channel_id=1, source_target_pairs={{1,0},{3,2},{5,4},{7,6},{9,8},{11,10},{13,12},{15,14},{17,16},{19,... | collective-permute-start | bytes 6291464 | tf_op jit(solution)/shard_map/ppermute | solution.py:100
  95.7 0.0 copy-done.2
  95.7 2.4 %convolution_convert_fusion = bf16[1024,512]{1,0:T(8,128)(2,1)S(1)} fusion(bf16[1024,2048]{1,0:T(8,128)(2,1)S(1)} %multiply_convert_fusion, bf16[2048,512]{1,0:T(8,128)(2,1)S(1)} %bitcast.24, bf16[2048,512]{1,0:T(8,128)(2,1)S(1)} %copy-done.2, pred[]{:T(512)S(6)} %eq.29), kind=kOutput, calls=%fused_computation.8 | convolution fusion | flops 2149056512 | bytes 9437185 | tf_op jit(solution)/shard_map/dot_general | solution.py:99
  98.0 1.3 collective-permute-start.6
  99.3 3.3 %collective-permute-done.6 = bf16[1024,512]{1,0:T(8,128)(2,1)S(1)} collective-permute-done((bf16[1024,512]{1,0:T(8,128)(2,1)S(1)}, bf16[1024,512]{1,0:T(8,128)(2,1)S(1)}, u32[]{:S(2)}, u32[]{:S(2)}) %collective-permute-start.6) | collective-permute-done | bytes 1048608 | tf_op jit(solution)/shard_map/ppermute | solution.py:101
  102.6 0.0 collective-permute-done.5
  102.6 1.0 fusion
  103.6 33.8 %all_to_all.16 = bf16[16,128,512]{2,1,0:T(8,128)(2,1)S(1)} all-to-all(bf16[16,128,512]{2,1,0:T(8,128)(2,1)S(1)} %bitcast.21), channel_id=1, replica_groups={{1,3,5,7,9,11,13,15,17,19,21,23,25,27,29,31},{33,35,37,39,41,43,45,47,4..., dimensions={0} | all-to-all | bytes 4194304 | tf_op jit(solution)/shard_map/all_to_all | solution.py:36
  137.3 0.3 reduce_sum.42
  137.6 2.3 %collective-permute-start.7 = (bf16[64,512]{1,0:T(8,128)(2,1)S(1)}, bf16[64,512]{1,0:T(8,128)(2,1)S(1)}, u32[]{:S(2)}, u32[]{:S(2)}) collective-permute-start(bf16[64,512]{1,0:T(8,128)(2,1)S(1)} %broadcast_select_fusion.5), channel_id=1, source_target_pairs={{0,1},{1,0},{2,3},{3,2},{4,5},{5,4},{6,7},{7,6},{8,9},{9,8},{10,11... | collective-permute-start | bytes 196616 | tf_op jit(solution)/shard_map/ppermute | solution.py:32
  140.0 0.9 collective-permute-done.7
  140.8 0.7 broadcast_select_fusion.3
  (15 shorter events, 0.2 us)
Async XLA Ops:
  0.6 50.4 %copy-start.3 = (s32[64]{0:T(128)S(1)}, s32[64]{0:T(128)}, u32[]{:S(2)}) copy-start(s32[64]{0:T(128)} %param.5) | copy-start | bytes 772
  1.5 9.7 %collective-permute-start = (bf16[64,512]{1,0:T(8,128)(2,1)S(1)}, bf16[64,512]{1,0:T(8,128)(2,1)S(1)}, u32[]{:S(2)}, u32[]{:S(2)}) collective-permute-start(bf16[64,512]{1,0:T(8,128)(2,1)S(1)} %broadcast_select_fusion.6), channel_id=1, source_target_pairs={{0,1},{1,0},{2,3},{3,2},{4,5},{5,4},{6,7},{7,6},{8,9},{9,8},{10,11... | collective-permute-start | bytes 196616 | tf_op jit(solution)/shard_map/ppermute | solution.py:32
  42.3 12.5 %collective-permute-start.1 = (bf16[2048,512]{1,0:T(8,128)(2,1)S(1)}, bf16[2048,512]{1,0:T(8,128)(2,1)S(1)}, u32[]{:S(2)}, u32[]{:S(2)}) collective-permute-start(bf16[2048,512]{1,0:T(8,128)(2,1)S(1)} %bitcast.22), channel_id=1, source_target_pairs={{0,1},{1,0},{2,3},{3,2},{4,5},{5,4},{6,7},{7,6},{8,9},{9,8},{10,11... | collective-permute-start | bytes 6291464 | tf_op jit(solution)/shard_map/ppermute | solution.py:32
  51.1 13.8 %collective-permute-start.3 = (s32[64]{0:T(128)S(1)}, s32[64]{0:T(128)S(1)}, u32[]{:S(2)}, u32[]{:S(2)}) collective-permute-start(s32[64]{0:T(128)S(1)} %copy-done.3), channel_id=1, source_target_pairs={{0,1},{1,0},{2,3},{3,2},{4,5},{5,4},{6,7},{7,6},{8,9},{9,8},{10,11... | collective-permute-start | bytes 776 | tf_op jit(solution)/shard_map/ppermute | solution.py:32
  54.8 2.6 %copy-start.1 = (bf16[2048,512]{1,0:T(8,128)(2,1)}, bf16[2048,512]{1,0:T(8,128)(2,1)S(1)}, u32[]{:S(2)}) copy-start(bf16[2048,512]{1,0:T(8,128)(2,1)S(1)} %collective-permute-done.1) | copy-start | bytes 6291460
  57.4 3.2 %copy-start = (f32[1024,2048]{1,0:T(8,128)}, f32[1024,2048]{1,0:T(8,128)S(1)}, u32[]{:S(2)}) copy-start(f32[1024,2048]{1,0:T(8,128)S(1)} %get-tuple-element.11) | copy-start | bytes 25165828
  62.6 3.1 %collective-permute-start.2 = (f32[2048]{0:T(1024)S(1)}, f32[2048]{0:T(1024)S(1)}, u32[]{:S(2)}, u32[]{:S(2)}) collective-permute-start(f32[2048]{0:T(1024)S(1)} %pad_select_fusion), channel_id=1, source_target_pairs={{0,1},{1,0},{2,3},{3,2},{4,5},{5,4},{6,7},{7,6},{8,9},{9,8},{10,11... | collective-permute-start | bytes 24584 | tf_op jit(solution)/shard_map/ppermute | solution.py:32
  66.4 14.6 %all-to-all-start.1 = ((f32[16,17,128]{2,1,0:T(8,128)}), f32[16,17,128]{2,1,0:T(8,128)S(1)}, u32[]{:S(2)}, u32[]{:S(2)}) async-start(f32[16,17,128]{2,1,0:T(8,128)} %broadcast_in_dim.16), calls=%async_computation.1 | async-start | bytes 393216 | tf_op jit(solution)/shard_map/all_to_all | solution.py:36
  81.1 3.1 %collective-permute-start.4 = (f32[2048]{0:T(1024)S(1)}, f32[2048]{0:T(1024)S(1)}, u32[]{:S(2)}, u32[]{:S(2)}) collective-permute-start(f32[2048]{0:T(1024)S(1)} %maximum_select_fusion.2), channel_id=1, source_target_pairs={{0,1},{1,0},{2,3},{3,2},{4,5},{5,4},{6,7},{7,6},{8,9},{9,8},{10,11... | collective-permute-start | bytes 24584 | tf_op jit(solution)/shard_map/ppermute | solution.py:32
  90.6 5.1 %copy-start.2 = (bf16[2048,512]{1,0:T(8,128)(2,1)S(1)}, bf16[2048,512]{1,0:T(8,128)(2,1)}, u32[]{:S(2)}) copy-start(bf16[2048,512]{1,0:T(8,128)(2,1)} %copy-done.1) | copy-start | bytes 6291460
  93.1 9.5 %collective-permute-start.5 = (bf16[2048,512]{1,0:T(8,128)(2,1)S(1)}, bf16[2048,512]{1,0:T(8,128)(2,1)S(1)}, u32[]{:S(2)}, u32[]{:S(2)}) collective-permute-start(bf16[2048,512]{1,0:T(8,128)(2,1)S(1)} %get-tuple-element.12), channel_id=1, source_target_pairs={{1,0},{3,2},{5,4},{7,6},{9,8},{11,10},{13,12},{15,14},{17,16},{19,... | collective-permute-start | bytes 6291464 | tf_op jit(solution)/shard_map/ppermute | solution.py:100
  98.0 4.6 %collective-permute-start.6 = (bf16[1024,512]{1,0:T(8,128)(2,1)S(1)}, bf16[1024,512]{1,0:T(8,128)(2,1)S(1)}, u32[]{:S(2)}, u32[]{:S(2)}) collective-permute-start(bf16[1024,512]{1,0:T(8,128)(2,1)S(1)} %convolution_convert_fusion), channel_id=1, source_target_pairs={{0,1},{2,3},{4,5},{6,7},{8,9},{10,11},{12,13},{14,15},{16,17},{18,... | collective-permute-start | bytes 3145736 | tf_op jit(solution)/shard_map/ppermute | solution.py:101
  137.6 3.2 %collective-permute-start.7 = (bf16[64,512]{1,0:T(8,128)(2,1)S(1)}, bf16[64,512]{1,0:T(8,128)(2,1)S(1)}, u32[]{:S(2)}, u32[]{:S(2)}) collective-permute-start(bf16[64,512]{1,0:T(8,128)(2,1)S(1)} %broadcast_select_fusion.5), channel_id=1, source_target_pairs={{0,1},{1,0},{2,3},{3,2},{4,5},{5,4},{6,7},{7,6},{8,9},{9,8},{10,11... | collective-permute-start | bytes 196616 | tf_op jit(solution)/shard_map/ppermute | solution.py:32

commit v2 on v0

v2 whole, which is shorter than its diff:
```python
import jax
import jax.numpy as jnp
from jax import lax
from jax.sharding import Mesh, PartitionSpec as P

TAU = 0.1
AX = "d"
NZ, NX, NY, NC = 8, 4, 8, 2
DEVICES = NZ * NX * NY * NC


def dev(z, x, y, c):
    return ((z * NX + x) * NY + y) * NC + c


PAIRS_M = ((0, 1), (2, 3))
PAIRS_T = ((0, 3), (1, 2))
ZS, XS, YS, CS = range(NZ), range(NX), range(NY), range(NC)
RING_Y = [[dev(z, x, y, c) for y in YS] for z in ZS for x in XS for c in CS]
RING_Z = [[dev(z, x, y, c) for z in ZS] for y in YS for x in XS for c in CS]
GROUP_M = [[dev(z, x, y, c) for x in p for y in YS] for z in ZS for p in PAIRS_M for c in CS]
GROUP_T = [[dev(z, x, y, c) for x in p for z in ZS] for y in YS for p in PAIRS_T for c in CS]
SWAP_C = [(i, i ^ 1) for i in range(DEVICES)]
SWAP_M = [
    (dev(z, x, y, c), dev(z, x ^ 1, y, c)) for z in ZS for x in XS for y in YS for c in CS
]
SWAP_T = [
    (dev(z, x, y, c), dev(z, 3 - x, y, c)) for z in ZS for x in XS for y in YS for c in CS
]


def swap(x, pairs):
    return lax.ppermute(x, AX, pairs)


def exchange(x, groups):
    return lax.all_to_all(x, AX, 0, 0, axis_index_groups=groups)


def spread(x, groups):
    return exchange(jnp.broadcast_to(x[None], (len(groups[0]), *x.shape)), groups)


def lse(x, axis):
    peak = jnp.max(x, axis=axis, keepdims=True)
    return jnp.squeeze(peak, axis) + jnp.log(jnp.sum(jnp.exp(x - peak), axis=axis))


def dot(a, b, dims):
    return lax.dot_general(a, b, (dims, ((), ())), preferred_element_type=jnp.float32)


def text_ids(x, y, core, n):
    shape = (NZ, 2, n)
    z = lax.broadcasted_iota(jnp.int32, shape, 0)
    xs = jnp.where(lax.broadcasted_iota(jnp.int32, shape, 1) == 0, x, 3 - x)
    k = lax.broadcasted_iota(jnp.int32, shape, 2)
    return ((((z * NX + xs) * NY + y) * NC + core) * n + k).reshape(1, -1)


def per_device(motion, text, pair_text):
    n, width = motion.shape
    d = lax.axis_index(AX)
    core, y, x = d % NC, d // NC % NY, d // (NC * NY) % NX
    second_m, second_t = x % 2 == 1, x >= 2

    def order_m(v):
        v = v.reshape(2, -1)
        return jnp.where(second_m, v[::-1], v).reshape(-1)

    def order_t(v):
        v = v.reshape(NZ, 2, -1)
        return jnp.where(second_t, v[:, ::-1], v).reshape(-1)

    text_pair = jnp.concatenate([text, swap(text, SWAP_T)])
    rows_own = spread(motion, RING_Y).reshape(NY * n, width)
    rows = jnp.concatenate([rows_own, swap(rows_own, SWAP_M)])
    cols_own = spread(text_pair, RING_Z).reshape(NZ * 2 * n, width)
    cols_sib = swap(cols_own, SWAP_C)
    half = NZ * 2 * n

    s_own = dot(rows, cols_own, ((1,), (1,))) / TAU
    s_sib = dot(rows, cols_sib, ((1,), (1,))) / TAU
    col_own, col_sib = lse(s_own, 0), lse(s_sib, 0)
    col_part = jnp.logaddexp(col_own, swap(col_sib, SWAP_C))
    col_lse = lse(spread(order_t(col_part).reshape(-1, 128), GROUP_T), 0).reshape(-1)
    col_lse = order_t(col_lse)
    col_lse_sib = swap(col_lse, SWAP_C)
    row_peak = jnp.maximum(jnp.max(s_own, axis=1), jnp.max(s_sib, axis=1))
    row_sum = jnp.sum(jnp.exp(s_own - row_peak[:, None]), axis=1) + jnp.sum(
        jnp.exp(s_sib - row_peak[:, None]), axis=1
    )
    row_part = order_m(row_peak + jnp.log(row_sum))
    pairs = jnp.concatenate([pair_text.astype(jnp.float32), jnp.zeros((128 - n,), jnp.float32)])
    stats = spread(jnp.concatenate([row_part, pairs]).reshape(-1, 128), GROUP_M)
    row_lse = order_m(lse(stats[:, :-1], 0).reshape(-1))
    pair_rows = order_m(stats[:, -1, :n].reshape(-1)).astype(jnp.int32)

    def weights_of(scores, stat, ids):
        positive = (pair_rows[:, None] == ids).astype(jnp.float32)
        return (
            (jnp.exp(scores - row_lse[:, None]) + jnp.exp(scores - stat[None, :]) - 2.0 * positive)
            / (2.0 * TAU)
        ).astype(jnp.bfloat16)

    w_own = weights_of(s_own, col_lse, text_ids(x, y, core, n))
    w_sib = weights_of(s_sib, col_lse_sib, text_ids(x, y, 1 - core, n))
    text_sib = swap(dot(w_sib, rows, ((0,), (0,))).astype(jnp.bfloat16), SWAP_C)
    motion_part = dot(w_own, cols_own, ((1,), (0,))) + dot(w_sib, cols_sib, ((1,), (0,)))
    motion_part = motion_part.astype(jnp.bfloat16).reshape(2, NY, n, width).transpose(1, 0, 2, 3)
    motion_sum = jnp.sum(exchange(motion_part, RING_Y).astype(jnp.float32), axis=0)
    motion_got = swap(motion_sum[1].astype(jnp.bfloat16), SWAP_M)
    motion_grad = (motion_sum[0] + motion_got.astype(jnp.float32)).astype(jnp.bfloat16)

    text_part = dot(w_own, rows, ((0,), (0,))) + text_sib.astype(jnp.float32)
    text_part = text_part.reshape(NZ, 2, n, width)
    text_got = swap(text_part[:, 1].astype(jnp.bfloat16), SWAP_T)
    text_part = (text_part[:, 0] + text_got.astype(jnp.float32)).astype(jnp.bfloat16)
    text_sum = jnp.sum(exchange(text_part, RING_Z).astype(jnp.float32), axis=0)
    return (motion_grad, text_sum.astype(jnp.bfloat16))


def solution(mesh):
    flat = Mesh(mesh.devices.reshape(DEVICES), (AX,))
    return jax.shard_map(
        per_device,
        mesh=flat,
        in_specs=(P(AX, None), P(AX, None), P(AX)),
        out_specs=(P(AX, None), P(AX, None)),
        check_vma=False,
    )
```

time: 653 us -> 198 us (0.30)
  waiting for transfers between devices: 418 us -> 66.2 us
  blocking collectives: 179 us -> 35.8 us
  starting transfers between devices: 0.16 us -> 60.4 us
  between operations: 14.5 us -> 1.15 us
    reduce_scatter x2 -> x0, waiting for transfers between devices: 302 us -> none  [the longest x1 224 us: per_device(): lax.psum_scatter(lax.dot_general(part, block_rows, (((0,), (0,)), ((), ()...]
    all_gather x2 -> x0, waiting for transfers between devices: 115 us -> none  [the longest x1 81.9 us: per_device(): block_text = lax.all_gather(text, 'row', axis=0, tiled=True)]
    pmax x2 -> x0, blocking collectives: 86.5 us -> none  [the longest x1 59 us: per_device(): col_peak = lax.pmax(jnp.max(scores, axis=0), 'row')]
    psum x2 -> x0, blocking collectives: 80.5 us -> none  [the longest x1 56.9 us: per_device(): lax.psum(jnp.sum(jnp.exp(scores - col_peak[None, :]), axis=0), 'row')]
    all_to_all x0 -> x5, waiting for transfers between devices: none -> 39.2 us  [exchange(): return lax.all_to_all(x, AX, 0, 0, axis_index_groups=groups)]
    all_to_all x0 -> x1, blocking collectives: none -> 35.8 us  [exchange(): return lax.all_to_all(x, AX, 0, 0, axis_index_groups=groups)]
    ppermute x0 -> x8, starting transfers between devices: none -> 34.8 us  [swap(): return lax.ppermute(x, AX, pairs)]
    ppermute x0 -> x8, waiting for transfers between devices: none -> 27 us  [swap(): return lax.ppermute(x, AX, pairs)]
  transfers between devices with their start and end apart: 4 -> 13, of which waited for: 4 -> 10; matrix products, arithmetic and copies ran while one was open for 1% -> 6% of each run, Pallas kernels for 0% -> 0%
where the time goes in v2:
time: 198 us; the launch traced here: 197 us
  waiting for transfers between devices  66.2 us (33%)
  starting transfers between devices  60.4 us (31%)
  blocking collectives  35.8 us (18%)
  other arithmetic  14.1 us (7%)
  matrix products  13.8 us (7%)
  local copies, waits for them, and re-layouts  5.37 us (3%)
    all_to_all x5, waiting for transfers between devices, exchange(): return lax.all_to_all(x, AX, 0, 0, axis_index_groups=groups)  39.2 us
    all_to_all x1, blocking collectives, exchange(): return lax.all_to_all(x, AX, 0, 0, axis_index_groups=groups)  35.8 us
    ppermute x8, starting transfers between devices, swap(): return lax.ppermute(x, AX, pairs)  34.8 us
    ppermute x8, waiting for transfers between devices, swap(): return lax.ppermute(x, AX, pairs)  27 us
    all_to_all x5, starting transfers between devices, exchange(): return lax.all_to_all(x, AX, 0, 0, axis_index_groups=groups)  25.6 us
    dot_general x6, matrix products, dot(): lax.dot_general(a, b, (dims, ((), ())), preferred_element_type=jnp.float32)  13.8 us
    convert_element_type x1, other arithmetic, weights_of(): return ((jnp.exp(scores - row_lse[:, None]) + jnp.exp(scores - stat[None,...  6.6 us
  transfers between devices with their start and end apart: 13, of which 10 were waited for; matrix products, arithmetic and copies ran while one was open for 6% of the time, Pallas kernels for 0%

profile of v2, /device:TPU:1, one launch (start us, length us, event | category | flops | bytes accessed | tf_op | source)
XLA Modules:
  0.0 196.8 jit_solution(16712131675351159876)
XLA Ops:
  0.6 0.0 copy-start.6
  0.6 5.2 %collective-permute-start.1 = (bf16[64,512]{1,0:T(8,128)(2,1)}, bf16[64,512]{1,0:T(8,128)(2,1)S(1)}, u32[]{:S(2)}, u32[]{:S(2)}) collective-permute-start(bf16[64,512]{1,0:T(8,128)(2,1)} %param.4), channel_id=1, source_target_pairs={{0,48},{1,49},{2,50},{3,51},{4,52},{5,53},{6,54},{7,55},{8,56},{9,... | collective-permute-start | bytes 196616 | tf_op jit(solution)/shard_map/ppermute | solution.py:33
  5.9 1.9 collective-permute-done.1
  7.7 0.8 pad_maximum_fusion.1
  8.6 0.1 broadcast_in_dim.25
  8.7 35.8 %all_to_all.30 = bf16[8,128,512]{2,1,0:T(8,128)(2,1)S(1)} all-to-all(bf16[8,128,512]{2,1,0:T(8,128)(2,1)S(1)} %broadcast_in_dim.25), channel_id=1, replica_groups={{0,64,128,192,256,320,384,448},{1,65,129,193,257,321,385,449},{16,80,14..., dimensions={0} | all-to-all | bytes 2097152 | tf_op jit(solution)/shard_map/all_to_all | solution.py:37
  44.5 1.7 broadcast_in_dim.22
  46.2 6.8 %all-to-all-start = ((bf16[8,64,512]{2,1,0:T(8,128)(2,1)}), bf16[8,64,512]{2,1,0:T(8,128)(2,1)S(1)}, u32[]{:S(2)}, u32[]{:S(2)}) async-start(bf16[8,64,512]{2,1,0:T(8,128)(2,1)} %broadcast_in_dim.22), calls=%async_computation | async-start | bytes 1048576 | tf_op jit(solution)/shard_map/all_to_all | solution.py:37
  53.0 6.0 %collective-permute-start.2 = (bf16[1024,512]{1,0:T(8,128)(2,1)S(1)}, bf16[1024,512]{1,0:T(8,128)(2,1)S(1)}, u32[]{:S(2)}, u32[]{:S(2)}) collective-permute-start(bf16[1024,512]{1,0:T(8,128)(2,1)S(1)} %bitcast.51), channel_id=1, source_target_pairs={{0,1},{1,0},{2,3},{3,2},{4,5},{5,4},{6,7},{7,6},{8,9},{9,8},{10,11... | collective-permute-start | bytes 3145736 | tf_op jit(solution)/shard_map/ppermute | solution.py:33
  59.0 6.9 %all-to-all-done = bf16[8,64,512]{2,1,0:T(8,128)(2,1)S(1)} async-done(((bf16[8,64,512]{2,1,0:T(8,128)(2,1)}), bf16[8,64,512]{2,1,0:T(8,128)(2,1)S(1)}, u32[]{:S(2)}, u32[]{:S(2)}) %all-to-all-start) | async-done | bytes 524320 | tf_op jit(solution)/shard_map/all_to_all | solution.py:37
  65.9 1.9 collective-permute-start
  67.9 0.0 copy-done.6
  67.9 0.1 iota_add_fusion.1
  68.0 0.1 reshape.137
  68.1 0.1 reshape.136
  68.2 7.7 %collective-permute-done = bf16[512,512]{1,0:T(8,128)(2,1)} collective-permute-done((bf16[512,512]{1,0:T(8,128)(2,1)S(1)}, bf16[512,512]{1,0:T(8,128)(2,1)}, u32[]{:S(2)}, u32[]{:S(2)}) %collective-permute-start) | collective-permute-done | bytes 524320 | tf_op jit(solution)/shard_map/ppermute | solution.py:33
  75.9 2.4 %multiply_reduce_fusion.3 = (f32[1024]{0:T(1024)S(1)}, f32[1024,1024]{1,0:T(8,128)S(1)}) fusion(bf16[1024,512]{1,0:T(8,128)(2,1)S(1)} %bitcast.52, bf16[512,512]{1,0:T(8,128)(2,1)} %collective-permute-done, bf16[512,512]{1,0:T(8,128)(2,1)S(1)} %bitcast.56), kind=kOutput, calls=%fused_computation.9 | convolution fusion | flops 1077935104 | bytes 6295552 | tf_op jit(solution)/shard_map/dot_general | solution.py:50
  78.3 0.0 collective-permute-done.2
  78.4 2.8 %multiply_reduce_fusion.1 = (f32[1024]{0:T(1024)S(1)}, f32[1024,1024]{1,0:T(8,128)S(1)}) fusion(bf16[1024,512]{1,0:T(8,128)(2,1)S(1)} %collective-permute-done.2, bf16[512,512]{1,0:T(8,128)(2,1)} %collective-permute-done, bf16[512,512]{1,0:T(8,128)(2,1)S(1)} %bitcast.57), kind=kOutput, calls=%fused_computation.7 | convolution fusion | flops 1077935104 | bytes 6295552 | tf_op jit(solution)/shard_map/dot_general | solution.py:50
  81.1 0.0 copy-start.1
  81.2 2.4 %exponential_reduce_fusion.2 = (f32[1024]{0:T(1024)S(1)}, f32[1024]{0:T(1024)S(1)}, f32[1024]{0:T(1024)S(1)}, f32[1024]{0:T(1024)S(1)}) fusion(f32[1024,1024]{1,0:T(8,128)S(1)} %get-tuple-element.15, f32[1024]{0:T(1024)S(1)} %max.12, f32[1024,1024]{1,0:T(8,128)S(1)} %get-tuple-element.13), kind=kLoop, calls=%fused_computation.4 | loop fusion | flops 8384512 | bytes 8409088 | tf_op jit(solution)/shard_map/reduce_sum | solution.py:90
  83.5 0.7 exponential_reduce_fusion
  84.3 8.6 %collective-permute-start.3 = (f32[1024]{0:T(1024)S(1)}, f32[1024]{0:T(1024)S(1)}, u32[]{:S(2)}, u32[]{:S(2)}) collective-permute-start(f32[1024]{0:T(1024)S(1)} %log_add_fusion.1), channel_id=1, source_target_pairs={{0,1},{1,0},{2,3},{3,2},{4,5},{5,4},{6,7},{7,6},{8,9},{9,8},{10,11... | collective-permute-start | bytes 12296 | tf_op jit(solution)/shard_map/ppermute | solution.py:33
  92.9 0.0 copy-done
  92.9 0.7 exponential_reduce_fusion.1
  93.6 0.1 collective-permute-done.3
  93.7 0.1 reshape.123
  93.8 0.1 rev.15
  94.0 0.1 broadcast_in_dim.53
  94.0 0.6 broadcast_in_dim.54
  94.7 8.2 %all-to-all-start.3 = ((f32[16,8,128]{2,1,0:T(8,128)}), f32[16,8,128]{2,1,0:T(8,128)S(1)}, u32[]{:S(2)}, u32[]{:S(2)}) async-start(f32[16,8,128]{2,1,0:T(8,128)} %broadcast_in_dim.54), calls=%async_computation.3 | async-start | bytes 131072 | tf_op jit(solution)/shard_map/all_to_all | solution.py:37
  102.9 0.1 concatenate.11
  103.0 8.5 %all-to-all-done.3 = f32[16,8,128]{2,1,0:T(8,128)S(1)} async-done(((f32[16,8,128]{2,1,0:T(8,128)}), f32[16,8,128]{2,1,0:T(8,128)S(1)}, u32[]{:S(2)}, u32[]{:S(2)}) %all-to-all-start.3) | async-done | bytes 65568 | tf_op jit(solution)/shard_map/all_to_all | solution.py:37
  111.5 0.7 broadcast_in_dim.52
  112.1 3.5 %all-to-all-start.2 = ((f32[16,9,128]{2,1,0:T(8,128)}), f32[16,9,128]{2,1,0:T(8,128)S(1)}, u32[]{:S(2)}, u32[]{:S(2)}) async-start(f32[16,9,128]{2,1,0:T(8,128)} %broadcast_in_dim.52), calls=%async_computation.2 | async-start | bytes 262144 | tf_op jit(solution)/shard_map/all_to_all | solution.py:37
  115.7 0.1 add.147
  115.8 0.1 sub.119
  115.9 3.7 %collective-permute-start.4 = (f32[1024]{0:T(1024)S(1)}, f32[1024]{0:T(1024)S(1)}, u32[]{:S(2)}, u32[]{:S(2)}) collective-permute-start(f32[1024]{0:T(1024)S(1)} %sub.119), channel_id=1, source_target_pairs={{0,1},{1,0},{2,3},{3,2},{4,5},{5,4},{6,7},{7,6},{8,9},{9,8},{10,11... | collective-permute-start | bytes 12296 | tf_op jit(solution)/shard_map/ppermute | solution.py:33
  119.6 3.5 %all-to-all-done.2 = f32[16,9,128]{2,1,0:T(8,128)S(1)} async-done(((f32[16,9,128]{2,1,0:T(8,128)}), f32[16,9,128]{2,1,0:T(8,128)S(1)}, u32[]{:S(2)}, u32[]{:S(2)}) %all-to-all-start.2) | async-done | bytes 73760 | tf_op jit(solution)/shard_map/all_to_all | solution.py:37
  123.1 0.1 reshape_reshape_squeeze.3
  123.3 0.1 rev.16
  123.4 0.1 rev.19
  123.6 0.0 collective-permute-done.4
  123.6 6.6 %multiply_convert_fusion = (bf16[1024,1024]{1,0:T(8,128)(2,1)S(1)}, bf16[1024,1024]{1,0:T(8,128)(2,1)S(1)}) fusion(f32[1024,1024]{1,0:T(8,128)} %copy-done.1, s32[1024]{0:T(1024)S(1)} %reshape.137, f32[1024]{0:T(1024)S(1)} %collective-permute-done.4, f32[1024]{0:T(1024)S(1)} %bitcast.67, s32[1024]{0:T(1024)S(1)} %bitcast.68, s32[1024]{0:T(1024)S(1)} %reshape.136, ...), kind=kLoop, calls=%fused_computation | loop fusion | flops 18874368 | bytes 12607488 | tf_op jit(solution)/shard_map/convert_element_type | solution.py:104
  130.2 3.3 %convolution_convert_fusion = bf16[1024,512]{1,0:T(8,128)(2,1)} fusion(bf16[1024,1024]{1,0:T(8,128)(2,1)S(1)} %get-tuple-element.8, bf16[512,512]{1,0:T(8,128)(2,1)} %collective-permute-done, bf16[512,512]{1,0:T(8,128)(2,1)S(1)} %bitcast.59), kind=kOutput, calls=%fused_computation.13 | convolution fusion | flops 1076363264 | bytes 4194304 | tf_op jit(solution)/shard_map/dot_general | solution.py:50
  133.5 4.7 %collective-permute-start.6 = (bf16[1024,512]{1,0:T(8,128)(2,1)}, bf16[1024,512]{1,0:T(8,128)(2,1)}, u32[]{:S(2)}, u32[]{:S(2)}) collective-permute-start(bf16[1024,512]{1,0:T(8,128)(2,1)} %convolution_convert_fusion), channel_id=1, source_target_pairs={{0,1},{1,0},{2,3},{3,2},{4,5},{5,4},{6,7},{7,6},{8,9},{9,8},{10,11... | collective-permute-start | bytes 3145736 | tf_op jit(solution)/shard_map/ppermute | solution.py:33
  138.3 1.3 fusion.8
  139.6 1.3 add_convert_fusion
  140.8 1.1 copy.21
  141.9 3.6 %all-to-all-start.4 = ((bf16[8,2,64,512]{3,2,1,0:T(8,128)(2,1)}), bf16[8,2,64,512]{3,2,1,0:T(8,128)(2,1)S(1)}, u32[]{:S(2)}, u32[]{:S(2)}) async-start(bf16[8,2,64,512]{3,2,1,0:T(8,128)(2,1)} %bitcast.42), calls=%async_computation.4 | async-start | bytes 2097152 | tf_op jit(solution)/shard_map/all_to_all | solution.py:37
  145.5 0.0 collective-permute-done.6
  145.5 2.8 %convert_add_fusion = f32[1024,512]{1,0:T(8,128)S(1)} fusion(bf16[1024,512]{1,0:T(8,128)(2,1)} %collective-permute-done.6, bf16[1024,1024]{1,0:T(8,128)(2,1)S(1)} %get-tuple-element.9, bf16[512,512]{1,0:T(8,128)(2,1)} %collective-permute-done, bf16[512,512]{1,0:T(8,128)(2,1)} %bitcast.58), kind=kOutput, calls=%fused_computation.10 | convolution fusion | flops 1076887552 | bytes 6291456 | tf_op jit(solution)/shard_map/dot_general | solution.py:50
  148.3 0.1 fusion.2
  148.4 2.0 %collective-permute-start.7 = (bf16[8,64,512]{2,1,0:T(8,128)(2,1)S(1)}, bf16[8,64,512]{2,1,0:T(8,128)(2,1)S(1)}, u32[]{:S(2)}, u32[]{:S(2)}) collective-permute-start(bf16[8,64,512]{2,1,0:T(8,128)(2,1)S(1)} %fusion.2), channel_id=1, source_target_pairs={{0,48},{1,49},{2,50},{3,51},{4,52},{5,53},{6,54},{7,55},{8,56},{9,... | collective-permute-start | bytes 1572872 | tf_op jit(solution)/shard_map/ppermute | solution.py:33
  150.4 14.6 %collective-permute-done.7 = bf16[8,64,512]{2,1,0:T(8,128)(2,1)S(1)} collective-permute-done((bf16[8,64,512]{2,1,0:T(8,128)(2,1)S(1)}, bf16[8,64,512]{2,1,0:T(8,128)(2,1)S(1)}, u32[]{:S(2)}, u32[]{:S(2)}) %collective-permute-start.7) | collective-permute-done | bytes 524320 | tf_op jit(solution)/shard_map/ppermute | solution.py:33
  165.1 1.0 fusion.1
  166.1 8.6 %all-to-all-done.4 = bf16[8,2,64,512]{3,2,1,0:T(8,128)(2,1)S(1)} async-done(((bf16[8,2,64,512]{3,2,1,0:T(8,128)(2,1)}), bf16[8,2,64,512]{3,2,1,0:T(8,128)(2,1)S(1)}, u32[]{:S(2)}, u32[]{:S(2)}) %all-to-all-start.4) | async-done | bytes 1048608 | tf_op jit(solution)/shard_map/all_to_all | solution.py:37
  174.7 3.5 %all-to-all-start.5 = ((bf16[8,64,512]{2,1,0:T(8,128)(2,1)}), bf16[8,64,512]{2,1,0:T(8,128)(2,1)S(1)}, u32[]{:S(2)}, u32[]{:S(2)}) async-start(bf16[8,64,512]{2,1,0:T(8,128)(2,1)} %fusion.1), calls=%async_computation.5 | async-start | bytes 1048576 | tf_op jit(solution)/shard_map/all_to_all | solution.py:37
  178.2 0.1 convert_reduce_fusion
  178.4 2.6 %collective-permute-start.5 = (bf16[64,512]{1,0:T(8,128)(2,1)S(1)}, bf16[64,512]{1,0:T(8,128)(2,1)S(1)}, u32[]{:S(2)}, u32[]{:S(2)}) collective-permute-start(bf16[64,512]{1,0:T(8,128)(2,1)S(1)} %fusion.5), channel_id=1, source_target_pairs={{0,16},{1,17},{2,18},{3,19},{4,20},{5,21},{6,22},{7,23},{8,24},{9,... | collective-permute-start | bytes 196616 | tf_op jit(solution)/shard_map/ppermute | solution.py:33
  181.0 2.7 %collective-permute-done.5 = bf16[64,512]{1,0:T(8,128)(2,1)S(1)} collective-permute-done((bf16[64,512]{1,0:T(8,128)(2,1)S(1)}, bf16[64,512]{1,0:T(8,128)(2,1)S(1)}, u32[]{:S(2)}, u32[]{:S(2)}) %collective-permute-start.5) | collective-permute-done | bytes 65568 | tf_op jit(solution)/shard_map/ppermute | solution.py:33
  183.7 0.6 fusion.4
  184.3 11.8 %all-to-all-done.5 = bf16[8,64,512]{2,1,0:T(8,128)(2,1)S(1)} async-done(((bf16[8,64,512]{2,1,0:T(8,128)(2,1)}), bf16[8,64,512]{2,1,0:T(8,128)(2,1)S(1)}, u32[]{:S(2)}, u32[]{:S(2)}) %all-to-all-start.5) | async-done | bytes 524320 | tf_op jit(solution)/shard_map/all_to_all | solution.py:37
  196.1 0.7 reduce_sum.82
  (39 shorter events, 0.4 us)
Async XLA Ops:
  0.6 67.3 %copy-start.6 = (s32[64]{0:T(128)S(1)}, s32[64]{0:T(128)}, u32[]{:S(2)}) copy-start(s32[64]{0:T(128)} %param.5) | copy-start | bytes 772
  0.6 7.1 %collective-permute-start.1 = (bf16[64,512]{1,0:T(8,128)(2,1)}, bf16[64,512]{1,0:T(8,128)(2,1)S(1)}, u32[]{:S(2)}, u32[]{:S(2)}) collective-permute-start(bf16[64,512]{1,0:T(8,128)(2,1)} %param.4), channel_id=1, source_target_pairs={{0,48},{1,49},{2,50},{3,51},{4,52},{5,53},{6,54},{7,55},{8,56},{9,... | collective-permute-start | bytes 196616 | tf_op jit(solution)/shard_map/ppermute | solution.py:33
  46.2 19.7 %all-to-all-start = ((bf16[8,64,512]{2,1,0:T(8,128)(2,1)}), bf16[8,64,512]{2,1,0:T(8,128)(2,1)S(1)}, u32[]{:S(2)}, u32[]{:S(2)}) async-start(bf16[8,64,512]{2,1,0:T(8,128)(2,1)} %broadcast_in_dim.22), calls=%async_computation | async-start | bytes 1048576 | tf_op jit(solution)/shard_map/all_to_all | solution.py:37
  53.0 25.3 %collective-permute-start.2 = (bf16[1024,512]{1,0:T(8,128)(2,1)S(1)}, bf16[1024,512]{1,0:T(8,128)(2,1)S(1)}, u32[]{:S(2)}, u32[]{:S(2)}) collective-permute-start(bf16[1024,512]{1,0:T(8,128)(2,1)S(1)} %bitcast.51), channel_id=1, source_target_pairs={{0,1},{1,0},{2,3},{3,2},{4,5},{5,4},{6,7},{7,6},{8,9},{9,8},{10,11... | collective-permute-start | bytes 3145736 | tf_op jit(solution)/shard_map/ppermute | solution.py:33
  65.9 12.4 %copy-start.2 = (bf16[8,64,512]{2,1,0:T(8,128)(2,1)}, bf16[8,64,512]{2,1,0:T(8,128)(2,1)S(1)}, u32[]{:S(2)}) copy-start(bf16[8,64,512]{2,1,0:T(8,128)(2,1)S(1)} %all-to-all-done) | copy-start | bytes 1572868
  65.9 10.0 %collective-permute-start = (bf16[512,512]{1,0:T(8,128)(2,1)S(1)}, bf16[512,512]{1,0:T(8,128)(2,1)}, u32[]{:S(2)}, u32[]{:S(2)}) collective-permute-start(bf16[512,512]{1,0:T(8,128)(2,1)S(1)} %bitcast.55), channel_id=1, source_target_pairs={{0,16},{1,17},{2,18},{3,19},{4,20},{5,21},{6,22},{7,23},{8,24},{9,... | collective-permute-start | bytes 1572872 | tf_op jit(solution)/shard_map/ppermute | solution.py:33
  78.3 14.6 %copy-start = (f32[1024,1024]{1,0:T(8,128)}, f32[1024,1024]{1,0:T(8,128)S(1)}, u32[]{:S(2)}) copy-start(f32[1024,1024]{1,0:T(8,128)S(1)} %get-tuple-element.13) | copy-start | bytes 12582916
  78.3 2.8 %copy-start.4 = (bf16[1024,512]{1,0:T(8,128)(2,1)}, bf16[1024,512]{1,0:T(8,128)(2,1)S(1)}, u32[]{:S(2)}) copy-start(bf16[1024,512]{1,0:T(8,128)(2,1)S(1)} %collective-permute-done.2) | copy-start | bytes 3145732
  81.1 2.4 %copy-start.1 = (f32[1024,1024]{1,0:T(8,128)}, f32[1024,1024]{1,0:T(8,128)S(1)}, u32[]{:S(2)}) copy-start(f32[1024,1024]{1,0:T(8,128)S(1)} %get-tuple-element.15) | copy-start | bytes 12582916
  84.3 9.4 %collective-permute-start.3 = (f32[1024]{0:T(1024)S(1)}, f32[1024]{0:T(1024)S(1)}, u32[]{:S(2)}, u32[]{:S(2)}) collective-permute-start(f32[1024]{0:T(1024)S(1)} %log_add_fusion.1), channel_id=1, source_target_pairs={{0,1},{1,0},{2,3},{3,2},{4,5},{5,4},{6,7},{7,6},{8,9},{9,8},{10,11... | collective-permute-start | bytes 12296 | tf_op jit(solution)/shard_map/ppermute | solution.py:33
  94.7 16.8 %all-to-all-start.3 = ((f32[16,8,128]{2,1,0:T(8,128)}), f32[16,8,128]{2,1,0:T(8,128)S(1)}, u32[]{:S(2)}, u32[]{:S(2)}) async-start(f32[16,8,128]{2,1,0:T(8,128)} %broadcast_in_dim.54), calls=%async_computation.3 | async-start | bytes 131072 | tf_op jit(solution)/shard_map/all_to_all | solution.py:37
  112.1 11.0 %all-to-all-start.2 = ((f32[16,9,128]{2,1,0:T(8,128)}), f32[16,9,128]{2,1,0:T(8,128)S(1)}, u32[]{:S(2)}, u32[]{:S(2)}) async-start(f32[16,9,128]{2,1,0:T(8,128)} %broadcast_in_dim.52), calls=%async_computation.2 | async-start | bytes 262144 | tf_op jit(solution)/shard_map/all_to_all | solution.py:37
  115.9 7.7 %collective-permute-start.4 = (f32[1024]{0:T(1024)S(1)}, f32[1024]{0:T(1024)S(1)}, u32[]{:S(2)}, u32[]{:S(2)}) collective-permute-start(f32[1024]{0:T(1024)S(1)} %sub.119), channel_id=1, source_target_pairs={{0,1},{1,0},{2,3},{3,2},{4,5},{5,4},{6,7},{7,6},{8,9},{9,8},{10,11... | collective-permute-start | bytes 12296 | tf_op jit(solution)/shard_map/ppermute | solution.py:33
  123.6 6.6 %copy-start.3 = (bf16[8,64,512]{2,1,0:T(8,128)(2,1)S(1)}, bf16[8,64,512]{2,1,0:T(8,128)(2,1)}, u32[]{:S(2)}) copy-start(bf16[8,64,512]{2,1,0:T(8,128)(2,1)} %copy-done.2) | copy-start | bytes 1572868
  133.5 11.9 %collective-permute-start.6 = (bf16[1024,512]{1,0:T(8,128)(2,1)}, bf16[1024,512]{1,0:T(8,128)(2,1)}, u32[]{:S(2)}, u32[]{:S(2)}) collective-permute-start(bf16[1024,512]{1,0:T(8,128)(2,1)} %convolution_convert_fusion), channel_id=1, source_target_pairs={{0,1},{1,0},{2,3},{3,2},{4,5},{5,4},{6,7},{7,6},{8,9},{9,8},{10,11... | collective-permute-start | bytes 3145736 | tf_op jit(solution)/shard_map/ppermute | solution.py:33
  138.3 1.3 copy-start.5
  141.9 32.8 %all-to-all-start.4 = ((bf16[8,2,64,512]{3,2,1,0:T(8,128)(2,1)}), bf16[8,2,64,512]{3,2,1,0:T(8,128)(2,1)S(1)}, u32[]{:S(2)}, u32[]{:S(2)}) async-start(bf16[8,2,64,512]{3,2,1,0:T(8,128)(2,1)} %bitcast.42), calls=%async_computation.4 | async-start | bytes 2097152 | tf_op jit(solution)/shard_map/all_to_all | solution.py:37
  148.4 16.7 %collective-permute-start.7 = (bf16[8,64,512]{2,1,0:T(8,128)(2,1)S(1)}, bf16[8,64,512]{2,1,0:T(8,128)(2,1)S(1)}, u32[]{:S(2)}, u32[]{:S(2)}) collective-permute-start(bf16[8,64,512]{2,1,0:T(8,128)(2,1)S(1)} %fusion.2), channel_id=1, source_target_pairs={{0,48},{1,49},{2,50},{3,51},{4,52},{5,53},{6,54},{7,55},{8,56},{9,... | collective-permute-start | bytes 1572872 | tf_op jit(solution)/shard_map/ppermute | solution.py:33
  174.7 21.4 %all-to-all-start.5 = ((bf16[8,64,512]{2,1,0:T(8,128)(2,1)}), bf16[8,64,512]{2,1,0:T(8,128)(2,1)S(1)}, u32[]{:S(2)}, u32[]{:S(2)}) async-start(bf16[8,64,512]{2,1,0:T(8,128)(2,1)} %fusion.1), calls=%async_computation.5 | async-start | bytes 1048576 | tf_op jit(solution)/shard_map/all_to_all | solution.py:37
  178.4 5.3 %collective-permute-start.5 = (bf16[64,512]{1,0:T(8,128)(2,1)S(1)}, bf16[64,512]{1,0:T(8,128)(2,1)S(1)}, u32[]{:S(2)}, u32[]{:S(2)}) collective-permute-start(bf16[64,512]{1,0:T(8,128)(2,1)S(1)} %fusion.5), channel_id=1, source_target_pairs={{0,16},{1,17},{2,18},{3,19},{4,20},{5,21},{6,22},{7,23},{8,24},{9,... | collective-permute-start | bytes 196616 | tf_op jit(solution)/shard_map/ppermute | solution.py:33

commit v3 on v1

v3 whole, which is shorter than its diff:
```python
import functools
import math

import jax
import jax.numpy as jnp
from jax import lax
from jax.experimental import pallas as pl
from jax.experimental.pallas import tpu as pltpu
from jax.sharding import Mesh, PartitionSpec as P

TAU = 0.1
SCALE = math.log2(math.e) / TAU
AX = "d"
NZ, NX, NY, NC = 8, 4, 8, 2
DEVICES = NZ * NX * NY * NC
G = 16
LANES = 128


def dev(z, x, y, c):
    return ((z * NX + x) * NY + y) * NC + c


MOTION_GROUPS = [
    [dev(z, x, y, 1) for x in pair for y in range(NY)]
    for z in range(NZ)
    for pair in ((0, 1), (2, 3))
]
TEXT_GROUPS = [
    [dev(z, x, y, 0) for x in pair for z in range(NZ)]
    for y in range(NY)
    for pair in ((0, 3), (1, 2))
]
GROUPS = MOTION_GROUPS + TEXT_GROUPS
CORES = [(i, i ^ 1) for i in range(DEVICES)]


def swap(x):
    return lax.ppermute(x, AX, CORES)


def exchange(x):
    return lax.all_to_all(x, AX, 0, 0, axis_index_groups=GROUPS)


def spread(x):
    return exchange(jnp.broadcast_to(x[None], (G, *x.shape)))


def dot(a, b, dims):
    return lax.dot_general(a, b, (dims, ((), ())), preferred_element_type=jnp.float32)


def stats_kernel(chunks, x_ref, y_ref, out_ref):
    x = x_ref[...]
    n = y_ref.shape[0] // chunks
    peaks, sums = [], []
    for c in range(chunks):
        s = dot(y_ref[c * n : (c + 1) * n, :], x, ((1,), (1,))) * SCALE
        peak = jnp.max(s, axis=0, keepdims=True)
        peaks.append(peak)
        sums.append(jnp.sum(jnp.exp2(s - peak), axis=0, keepdims=True))
    peak = functools.reduce(jnp.maximum, peaks)
    total = sum(jnp.exp2(a - peak) * b for a, b in zip(peaks, sums))
    out_ref[0] = peak + jnp.log2(total)


def block_stats(x, y, block=1024, chunks=8):
    rows, width = x.shape
    steps = rows // block
    out = pl.pallas_call(
        functools.partial(stats_kernel, chunks),
        grid=(steps,),
        in_specs=[
            pl.BlockSpec((block, width), lambda i: (i, 0)),
            pl.BlockSpec(y.shape, lambda i: (0, 0)),
        ],
        out_specs=pl.BlockSpec((1, 1, block), lambda i: (i, 0, 0)),
        out_shape=jax.ShapeDtypeStruct((steps, 1, block), jnp.float32),
        compiler_params=pltpu.CompilerParams(vmem_limit_bytes=40 << 20),
        name="block_stats",
    )(x, y)
    return out.reshape(rows // LANES, LANES)


def columns(ref, first, count):
    return jnp.concatenate(
        [
            jnp.transpose(jnp.broadcast_to(ref[pl.ds(first + r, 1), :], (LANES, LANES)))
            for r in range(count)
        ]
    )


def grads_kernel(x_ref, y_ref, lx_ref, kx_ref, ly_ref, ky_ref, out_ref):
    count = x_ref.shape[0] // LANES
    first = pl.program_id(0) * count
    lx, kx = columns(lx_ref, first, count), columns(kx_ref, first, count)
    y = y_ref[...]
    scores = dot(x_ref[...], y, ((1,), (1,)))
    weights = []
    for r in range(y.shape[0] // LANES):
        s = scores[:, r * LANES : (r + 1) * LANES] * SCALE
        w = jnp.exp2(s - lx) + jnp.exp2(s - ly_ref[r : r + 1, :])
        w = jnp.where(kx == ky_ref[r : r + 1, :], w - 2.0, w) * (0.5 / TAU)
        weights.append(w.astype(jnp.bfloat16))
    out_ref[...] = dot(jnp.concatenate(weights, axis=1), y, ((1,), (0,))).astype(jnp.bfloat16)


def block_grads(x, y, lx, kx, ly, ky, block=1024):
    rows, width = x.shape
    whole = pl.BlockSpec((rows // LANES, LANES), lambda i: (0, 0))
    return pl.pallas_call(
        grads_kernel,
        grid=(rows // block,),
        in_specs=[
            pl.BlockSpec((block, width), lambda i: (i, 0)),
            pl.BlockSpec(y.shape, lambda i: (0, 0)),
            whole,
            whole,
            whole,
            whole,
        ],
        out_specs=pl.BlockSpec((block, width), lambda i: (i, 0)),
        out_shape=jax.ShapeDtypeStruct(x.shape, jnp.bfloat16),
        compiler_params=pltpu.CompilerParams(vmem_limit_bytes=40 << 20),
        name="block_grads",
    )(x, y, lx, kx, ly, ky)


def per_device(motion, text, pair_text):
    n, width = motion.shape
    d = lax.axis_index(AX)
    is_text = d % NC == 0
    got = swap(jnp.where(is_text, motion, text))
    mine = jnp.where(is_text, jnp.concatenate([text, got]), jnp.concatenate([got, motion]))
    x = spread(mine).reshape(G * NC * n, width)
    y = swap(x)
    pair_got = swap(pair_text)
    ids = d // NC * (NC * n) + lax.iota(jnp.int32, NC * n)
    key = jnp.where(is_text, ids, jnp.concatenate([pair_got, pair_text])).astype(jnp.float32)
    part = block_stats(x, y)
    stats = spread(jnp.concatenate([part, key[None]]))
    parts, kx = stats[:, :G], stats[:, G]
    peak = jnp.max(parts, axis=0)
    lx = peak + jnp.log2(jnp.sum(jnp.exp2(parts - peak), axis=0))
    other = swap(jnp.concatenate([lx, kx]))
    grad_part = block_grads(x, y, lx, kx, other[:G], other[G:])
    grads = exchange(grad_part.reshape(G, NC * n, width))
    grad = jnp.sum(grads.astype(jnp.float32), axis=0).astype(jnp.bfloat16)
    grad_got = swap(jnp.where(is_text, grad[n:], grad[:n]))
    motion_grad = jnp.where(is_text, grad_got, grad[n:])
    text_grad = jnp.where(is_text, grad[:n], grad_got)
    return (motion_grad, text_grad)


def solution(mesh):
    flat = Mesh(mesh.devices.reshape(DEVICES), (AX,))
    return jax.shard_map(
        per_device,
        mesh=flat,
        in_specs=(P(AX, None), P(AX, None), P(AX)),
        out_specs=(P(AX, None), P(AX, None)),
        check_vma=False,
    )
```

time: 142 us -> 130 us (0.915)
  Pallas kernels: 0 us -> 18.3 us
  blocking collectives: 63.8 us -> 78.4 us
  starting transfers between devices: 37.1 us -> 24.1 us
  other arithmetic: 14.6 us -> 2.88 us
  waiting for transfers between devices: 15.8 us -> 4.44 us
  matrix products: 7.21 us -> 0 us
  local copies, waits for them, and re-layouts: 2 us -> 0.23 us
    pallas_call x0 -> x2, Pallas kernels: none -> 18.3 us  [the longest x1 11.5 us: block_grads(): pl.pallas_call(grads_kernel, grid=(rows // block,), in_specs=[pl.BlockSpe...]
    all_to_all x2 -> x3, blocking collectives: 63.8 us -> 78.4 us  [exchange(): return lax.all_to_all(x, AX, 0, 0, axis_index_groups=GROUPS)]
    all_to_all x1 -> x0, waiting for transfers between devices: 7.55 us -> none  [exchange(): return lax.all_to_all(x, AX, 0, 0, axis_index_groups=GROUPS)]
    dot_general x3 -> x0, matrix products: 7.21 us -> none  [the longest x1 2.46 us: per_device(): lax.dot_general(weights, rows, (((0,), (0,)), ((), ())), preferred_elemen...]
    all_to_all x1 -> x0, starting transfers between devices: 6.93 us -> none  [exchange(): return lax.all_to_all(x, AX, 0, 0, axis_index_groups=GROUPS)]
    convert_element_type x3 -> x1, other arithmetic: 6.48 us -> 0.08 us  [per_device(): jnp.where(is_text, ids, jnp.concatenate([pair_got, pair_text]))]
    ppermute x8 -> x5, starting transfers between devices: 30.2 us -> 24.1 us  [swap(): return lax.ppermute(x, AX, CORES)]
    reduce_sum x3 -> x1, other arithmetic: 4.13 us -> 0.04 us  [per_device(): lx = peak + jnp.log2(jnp.sum(jnp.exp2(parts - peak), axis=0))]
  transfers between devices with their start and end apart: 9 -> 5, of which waited for: 7 -> 5; matrix products, arithmetic and copies ran while one was open for 6% -> 0% of each run, Pallas kernels for 0% -> 0%
where the time goes in v3:
time: 130 us; the launch traced here: 129 us
  blocking collectives  78.4 us (60%)
  starting transfers between devices  24.1 us (19%)
  Pallas kernels  18.3 us (14%)
  waiting for transfers between devices  4.44 us (3%)
  other arithmetic  2.88 us (2%)
    all_to_all x3, blocking collectives, exchange(): return lax.all_to_all(x, AX, 0, 0, axis_index_groups=GROUPS)  78.4 us
    ppermute x5, starting transfers between devices, swap(): return lax.ppermute(x, AX, CORES)  24.1 us
    pallas_call x1, Pallas kernels, block_grads(): pl.pallas_call(grads_kernel, grid=(rows // block,), in_specs=[pl.BlockSpe...  11.5 us
    pallas_call x1, Pallas kernels, block_stats(): pl.pallas_call(functools.partial(stats_kernel, chunks), grid=(steps,), in...  6.77 us
    ppermute x5, waiting for transfers between devices, swap(): return lax.ppermute(x, AX, CORES)  4.44 us
  transfers between devices with their start and end apart: 5, of which 5 were waited for; matrix products, arithmetic and copies ran while one was open for 0% of the time, Pallas kernels for 0%

profile of v3, /device:TPU:1, one launch (start us, length us, event | category | flops | bytes accessed | tf_op | source)
XLA Modules:
  0.0 129.1 jit_solution(10602346536429926121)
XLA Ops:
  0.6 0.9 broadcast_select_fusion.3
  1.5 8.8 %collective-permute-start = (bf16[64,512]{1,0:T(8,128)(2,1)S(1)}, bf16[64,512]{1,0:T(8,128)(2,1)S(1)}, u32[]{:S(2)}, u32[]{:S(2)}) collective-permute-start(bf16[64,512]{1,0:T(8,128)(2,1)S(1)} %broadcast_select_fusion.3), channel_id=1, source_target_pairs={{0,1},{1,0},{2,3},{3,2},{4,5},{5,4},{6,7},{7,6},{8,9},{9,8},{10,11... | collective-permute-start | bytes 196616 | tf_op jit(solution)/shard_map/ppermute | solution.py:39
  10.3 0.9 collective-permute-done
  11.2 0.9 maximum_select_fusion
  12.1 0.2 broadcast_in_dim.4
  12.3 0.0 copy-start
  12.3 30.0 %all_to_all.15 = bf16[16,128,512]{2,1,0:T(8,128)(2,1)S(1)} all-to-all(bf16[16,128,512]{2,1,0:T(8,128)(2,1)S(1)} %broadcast_in_dim.4), channel_id=1, replica_groups={{1,3,5,7,9,11,13,15,17,19,21,23,25,27,29,31},{33,35,37,39,41,43,45,47,4..., dimensions={0} | all-to-all | bytes 4194304 | tf_op jit(solution)/shard_map/all_to_all | solution.py:43
  42.3 8.8 %collective-permute-start.1 = (bf16[2048,512]{1,0:T(8,128)(2,1)S(1)}, bf16[2048,512]{1,0:T(8,128)(2,1)}, u32[]{:S(2)}, u32[]{:S(2)}) collective-permute-start(bf16[2048,512]{1,0:T(8,128)(2,1)S(1)} %bitcast.8), channel_id=1, source_target_pairs={{0,1},{1,0},{2,3},{3,2},{4,5},{5,4},{6,7},{7,6},{8,9},{9,8},{10,11... | collective-permute-start | bytes 6291464 | tf_op jit(solution)/shard_map/ppermute | solution.py:39
  51.1 0.0 copy-done
  51.1 1.9 %collective-permute-start.2 = (s32[64]{0:T(128)S(1)}, s32[64]{0:T(128)S(1)}, u32[]{:S(2)}, u32[]{:S(2)}) collective-permute-start(s32[64]{0:T(128)S(1)} %copy-done), channel_id=1, source_target_pairs={{0,1},{1,0},{2,3},{3,2},{4,5},{5,4},{6,7},{7,6},{8,9},{9,8},{10,11... | collective-permute-start | bytes 776 | tf_op jit(solution)/shard_map/ppermute | solution.py:39
  53.0 1.8 %collective-permute-done.2 = s32[64]{0:T(128)S(1)} collective-permute-done((s32[64]{0:T(128)S(1)}, s32[64]{0:T(128)S(1)}, u32[]{:S(2)}, u32[]{:S(2)}) %collective-permute-start.2) | collective-permute-done | bytes 288 | tf_op jit(solution)/shard_map/ppermute | solution.py:39
  54.8 0.1 fusion
  54.9 0.1 collective-permute-done.1.y_ref
  55.0 6.8 %block_stats.1 = f32[2,1,1024]{2,1,0:T(1,128)S(1)} custom-call(bf16[2048,512]{1,0:T(8,128)(2,1)S(1)} %bitcast.9, bf16[2048,512]{1,0:T(8,128)(2,1)} %collective-permute-done.1.y_ref), custom_call_target="tpu_custom_call" | custom-call | tf_op jit(solution)/shard_map/block_stats/pallas_call | solution.py:71
  61.8 14.4 %all_to_all.16 = f32[16,17,128]{2,1,0:T(8,128)S(1)} all-to-all(f32[16,17,128]{2,1,0:T(8,128)S(1)} %broadcast_in_dim.5), channel_id=1, replica_groups={{1,3,5,7,9,11,13,15,17,19,21,23,25,27,29,31},{33,35,37,39,41,43,45,47,4..., dimensions={0} | all-to-all | bytes 278528 | tf_op jit(solution)/shard_map/all_to_all | solution.py:43
  76.2 2.3 %collective-permute-start.3 = (f32[32,128]{1,0:T(8,128)S(1)}, f32[32,128]{1,0:T(8,128)S(1)}, u32[]{:S(2)}, u32[]{:S(2)}) collective-permute-start(f32[32,128]{1,0:T(8,128)S(1)} %pad_maximum_fusion), channel_id=1, source_target_pairs={{0,1},{1,0},{2,3},{3,2},{4,5},{5,4},{6,7},{7,6},{8,9},{9,8},{10,11... | collective-permute-start | bytes 49160 | tf_op jit(solution)/shard_map/ppermute | solution.py:39
  78.5 0.8 collective-permute-done.3
  79.4 11.5 %block_grads.1 = bf16[2048,512]{1,0:T(8,128)(2,1)S(1)} custom-call(bf16[2048,512]{1,0:T(8,128)(2,1)S(1)} %bitcast.10, bf16[2048,512]{1,0:T(8,128)(2,1)} %collective-permute-done.1.y_ref, f32[16,128]{1,0:T(8,128)S(1)} %multiply_add_fusion.lx_ref, f32[16,128]{1,0:T(8,128)S(1)} %bitcast.13, f32[16,128]{1,0:T(8,128)S(1)} %get-tuple-element.5.ly_ref, ...), custom_call_target="tpu_custom_call" | custom-call | tf_op jit(solution)/shard_map/block_grads/pallas_call | solution.py:113
  90.9 34.0 %all_to_all.17 = bf16[16,128,512]{2,1,0:T(8,128)(2,1)S(1)} all-to-all(bf16[16,128,512]{2,1,0:T(8,128)(2,1)S(1)} %bitcast.11), channel_id=1, replica_groups={{1,3,5,7,9,11,13,15,17,19,21,23,25,27,29,31},{33,35,37,39,41,43,45,47,4..., dimensions={0} | all-to-all | bytes 4194304 | tf_op jit(solution)/shard_map/all_to_all | solution.py:43
  124.9 0.3 reduce_sum.22
  125.2 2.3 %collective-permute-start.4 = (bf16[64,512]{1,0:T(8,128)(2,1)S(1)}, bf16[64,512]{1,0:T(8,128)(2,1)S(1)}, u32[]{:S(2)}, u32[]{:S(2)}) collective-permute-start(bf16[64,512]{1,0:T(8,128)(2,1)S(1)} %broadcast_select_fusion.2), channel_id=1, source_target_pairs={{0,1},{1,0},{2,3},{3,2},{4,5},{5,4},{6,7},{7,6},{8,9},{9,8},{10,11... | collective-permute-start | bytes 196616 | tf_op jit(solution)/shard_map/ppermute | solution.py:39
  127.5 0.9 collective-permute-done.4
  128.4 0.7 broadcast_select_fusion
  (9 shorter events, 0.1 us)
Async XLA Ops:
  1.5 9.7 %collective-permute-start = (bf16[64,512]{1,0:T(8,128)(2,1)S(1)}, bf16[64,512]{1,0:T(8,128)(2,1)S(1)}, u32[]{:S(2)}, u32[]{:S(2)}) collective-permute-start(bf16[64,512]{1,0:T(8,128)(2,1)S(1)} %broadcast_select_fusion.3), channel_id=1, source_target_pairs={{0,1},{1,0},{2,3},{3,2},{4,5},{5,4},{6,7},{7,6},{8,9},{9,8},{10,11... | collective-permute-start | bytes 196616 | tf_op jit(solution)/shard_map/ppermute | solution.py:39
  12.3 38.8 %copy-start = (s32[64]{0:T(128)S(1)}, s32[64]{0:T(128)}, u32[]{:S(2)}) copy-start(s32[64]{0:T(128)} %param.5) | copy-start | bytes 772
  42.3 12.7 %collective-permute-start.1 = (bf16[2048,512]{1,0:T(8,128)(2,1)S(1)}, bf16[2048,512]{1,0:T(8,128)(2,1)}, u32[]{:S(2)}, u32[]{:S(2)}) collective-permute-start(bf16[2048,512]{1,0:T(8,128)(2,1)S(1)} %bitcast.8), channel_id=1, source_target_pairs={{0,1},{1,0},{2,3},{3,2},{4,5},{5,4},{6,7},{7,6},{8,9},{9,8},{10,11... | collective-permute-start | bytes 6291464 | tf_op jit(solution)/shard_map/ppermute | solution.py:39
  51.1 3.8 %collective-permute-start.2 = (s32[64]{0:T(128)S(1)}, s32[64]{0:T(128)S(1)}, u32[]{:S(2)}, u32[]{:S(2)}) collective-permute-start(s32[64]{0:T(128)S(1)} %copy-done), channel_id=1, source_target_pairs={{0,1},{1,0},{2,3},{3,2},{4,5},{5,4},{6,7},{7,6},{8,9},{9,8},{10,11... | collective-permute-start | bytes 776 | tf_op jit(solution)/shard_map/ppermute | solution.py:39
  76.2 3.1 %collective-permute-start.3 = (f32[32,128]{1,0:T(8,128)S(1)}, f32[32,128]{1,0:T(8,128)S(1)}, u32[]{:S(2)}, u32[]{:S(2)}) collective-permute-start(f32[32,128]{1,0:T(8,128)S(1)} %pad_maximum_fusion), channel_id=1, source_target_pairs={{0,1},{1,0},{2,3},{3,2},{4,5},{5,4},{6,7},{7,6},{8,9},{9,8},{10,11... | collective-permute-start | bytes 49160 | tf_op jit(solution)/shard_map/ppermute | solution.py:39
  125.2 3.2 %collective-permute-start.4 = (bf16[64,512]{1,0:T(8,128)(2,1)S(1)}, bf16[64,512]{1,0:T(8,128)(2,1)S(1)}, u32[]{:S(2)}, u32[]{:S(2)}) collective-permute-start(bf16[64,512]{1,0:T(8,128)(2,1)S(1)} %broadcast_select_fusion.2), channel_id=1, source_target_pairs={{0,1},{1,0},{2,3},{3,2},{4,5},{5,4},{6,7},{7,6},{8,9},{9,8},{10,11... | collective-permute-start | bytes 196616 | tf_op jit(solution)/shard_map/ppermute | solution.py:39

commit v4 on v3

--- a/solution.py
+++ b/solution.py
@@ -73,7 +73,7 @@
         grid=(steps,),
         in_specs=[
             pl.BlockSpec((block, width), lambda i: (i, 0)),
-            pl.BlockSpec(y.shape, lambda i: (0, 0)),
+            pl.BlockSpec(memory_space=pltpu.VMEM),
         ],
         out_specs=pl.BlockSpec((1, 1, block), lambda i: (i, 0, 0)),
         out_shape=jax.ShapeDtypeStruct((steps, 1, block), jnp.float32),
@@ -92,40 +92,68 @@
     )
 
 
-def grads_kernel(x_ref, y_ref, lx_ref, kx_ref, ly_ref, ky_ref, out_ref):
-    count = x_ref.shape[0] // LANES
-    first = pl.program_id(0) * count
-    lx, kx = columns(lx_ref, first, count), columns(kx_ref, first, count)
+VMEM = pl.BlockSpec(memory_space=pltpu.VMEM)
+
+
+def scores_kernel(block, x_ref, y_ref, out_ref):
     y = y_ref[...]
-    scores = dot(x_ref[...], y, ((1,), (1,)))
+    for i in range(0, x_ref.shape[0], block):
+        out_ref[i : i + block, :] = dot(x_ref[i : i + block, :], y, ((1,), (1,))) * SCALE
+
+
+def block_scores(x, y, block=512):
+    rows, width = x.shape
+    return pl.pallas_call(
+        functools.partial(scores_kernel, block),
+        in_specs=[VMEM, VMEM],
+        out_specs=VMEM,
+        out_shape=pltpu.VMEM((rows, y.shape[0]), jnp.float32),
+        compiler_params=pltpu.CompilerParams(vmem_limit_bytes=20 << 20),
+        cost_estimate=pl.CostEstimate(
+            flops=2 * rows * y.shape[0] * width,
+            bytes_accessed=4 * rows * y.shape[0] + 4 * rows * width,
+            transcendentals=0,
+        ),
+        name="block_scores",
+    )(x, y)
+
+
+def grads_kernel(s_ref, y_ref, lx_ref, kx_ref, ly_ref, ky_ref, out_ref):
+    block = out_ref.shape[0]
+    count = block // LANES
+    step = pl.program_id(0)
+    lx, kx = columns(lx_ref, step * count, count), columns(kx_ref, step * count, count)
+    rows = pl.ds(pl.multiple_of(step * block, block), block)
     weights = []
-    for r in range(y.shape[0] // LANES):
-        s = scores[:, r * LANES : (r + 1) * LANES] * SCALE
+    for r in range(s_ref.shape[1] // LANES):
+        s = s_ref[rows, r * LANES : (r + 1) * LANES]
         w = jnp.exp2(s - lx) + jnp.exp2(s - ly_ref[r : r + 1, :])
         w = jnp.where(kx == ky_ref[r : r + 1, :], w - 2.0, w) * (0.5 / TAU)
         weights.append(w.astype(jnp.bfloat16))
-    out_ref[...] = dot(jnp.concatenate(weights, axis=1), y, ((1,), (0,))).astype(jnp.bfloat16)
+    w = jnp.concatenate(weights, axis=1)
+    out_ref[...] = dot(w, y_ref[...], ((1,), (0,))).astype(jnp.bfloat16)
 
 
-def block_grads(x, y, lx, kx, ly, ky, block=1024):
-    rows, width = x.shape
+def block_grads(scores, y, lx, kx, ly, ky, block=1024):
+    rows = scores.shape[0]
+    width = y.shape[1]
     whole = pl.BlockSpec((rows // LANES, LANES), lambda i: (0, 0))
     return pl.pallas_call(
         grads_kernel,
         grid=(rows // block,),
         in_specs=[
-            pl.BlockSpec((block, width), lambda i: (i, 0)),
-            pl.BlockSpec(y.shape, lambda i: (0, 0)),
+            VMEM,
+            VMEM,
             whole,
             whole,
             whole,
             whole,
         ],
         out_specs=pl.BlockSpec((block, width), lambda i: (i, 0)),
-        out_shape=jax.ShapeDtypeStruct(x.shape, jnp.bfloat16),
-        compiler_params=pltpu.CompilerParams(vmem_limit_bytes=40 << 20),
+        out_shape=jax.ShapeDtypeStruct((rows, width), jnp.bfloat16),
+        compiler_params=pltpu.CompilerParams(vmem_limit_bytes=28 << 20),
         name="block_grads",
-    )(x, y, lx, kx, ly, ky)
+    )(scores, y, lx, kx, ly, ky)
 
 
 def per_device(motion, text, pair_text):
@@ -145,12 +173,12 @@
     peak = jnp.max(parts, axis=0)
     lx = peak + jnp.log2(jnp.sum(jnp.exp2(parts - peak), axis=0))
     other = swap(jnp.concatenate([lx, kx]))
-    grad_part = block_grads(x, y, lx, kx, other[:G], other[G:])
+    grad_part = block_grads(block_scores(x, y), y, lx, kx, other[:G], other[G:])
     grads = exchange(grad_part.reshape(G, NC * n, width))
     grad = jnp.sum(grads.astype(jnp.float32), axis=0).astype(jnp.bfloat16)
-    grad_got = swap(jnp.where(is_text, grad[n:], grad[:n]))
-    motion_grad = jnp.where(is_text, grad_got, grad[n:])
-    text_grad = jnp.where(is_text, grad[:n], grad_got)
+    grad_got = swap(grad)
+    motion_grad = jnp.where(is_text, grad_got[:n], grad[n:])
+    text_grad = jnp.where(is_text, grad[:n], grad_got[n:])
     return (motion_grad, text_grad)
 
 

time: 130 us -> 129 us (level)
    pallas_call x1 -> x2, Pallas kernels: 11.5 us -> 11.8 us  [the longest x1 6.15 us: block_scores(): pl.pallas_call(functools.partial(scores_kernel, block), in_specs=[VMEM, V...]
  transfers between devices with their start and end apart: 5 -> 5, of which waited for: 5 -> 4; matrix products, arithmetic and copies ran while one was open for 0% -> 0% of each run, Pallas kernels for 0% -> 5%
where the time goes in v4:
time: 129 us; the launch traced here: 128 us
  blocking collectives  79 us (61%)
  starting transfers between devices  23.5 us (18%)
  Pallas kernels  18.2 us (14%)
  waiting for transfers between devices  3.79 us (3%)
  other arithmetic  2.87 us (2%)
    all_to_all x3, blocking collectives, exchange(): return lax.all_to_all(x, AX, 0, 0, axis_index_groups=GROUPS)  79 us
    ppermute x5, starting transfers between devices, swap(): return lax.ppermute(x, AX, CORES)  23.5 us
    pallas_call x1, Pallas kernels, block_stats(): pl.pallas_call(functools.partial(stats_kernel, chunks), grid=(steps,), in...  6.43 us
    pallas_call x1, Pallas kernels, block_scores(): pl.pallas_call(functools.partial(scores_kernel, block), in_specs=[VMEM, V...  6.15 us
    pallas_call x1, Pallas kernels, block_grads(): pl.pallas_call(grads_kernel, grid=(rows // block,), in_specs=[VMEM, VMEM,...  5.65 us
    ppermute x5, waiting for transfers between devices, swap(): return lax.ppermute(x, AX, CORES)  3.79 us
  transfers between devices with their start and end apart: 5, of which 4 were waited for; matrix products, arithmetic and copies ran while one was open for 0% of the time, Pallas kernels for 5%

profile of v4, /device:TPU:1, one launch (start us, length us, event | category | flops | bytes accessed | tf_op | source)
XLA Modules:
  0.0 128.5 jit_solution(12595188290301302234)
XLA Ops:
  0.6 0.9 broadcast_select_fusion
  1.5 8.8 %collective-permute-start = (bf16[64,512]{1,0:T(8,128)(2,1)S(1)}, bf16[64,512]{1,0:T(8,128)(2,1)S(1)}, u32[]{:S(2)}, u32[]{:S(2)}) collective-permute-start(bf16[64,512]{1,0:T(8,128)(2,1)S(1)} %broadcast_select_fusion), channel_id=1, source_target_pairs={{0,1},{1,0},{2,3},{3,2},{4,5},{5,4},{6,7},{7,6},{8,9},{9,8},{10,11... | collective-permute-start | bytes 196616 | tf_op jit(solution)/shard_map/ppermute | solution.py:39
  10.3 0.9 collective-permute-done
  11.2 0.9 maximum_select_fusion
  12.1 0.2 broadcast_in_dim.4
  12.3 0.0 copy-start
  12.3 30.7 %all_to_all.15 = bf16[16,128,512]{2,1,0:T(8,128)(2,1)} all-to-all(bf16[16,128,512]{2,1,0:T(8,128)(2,1)S(1)} %broadcast_in_dim.4), channel_id=1, replica_groups={{1,3,5,7,9,11,13,15,17,19,21,23,25,27,29,31},{33,35,37,39,41,43,45,47,4..., dimensions={0} | all-to-all | bytes 4194304 | tf_op jit(solution)/shard_map/all_to_all | solution.py:43
  43.0 8.2 %collective-permute-start.1 = (bf16[2048,512]{1,0:T(8,128)(2,1)}, bf16[2048,512]{1,0:T(8,128)(2,1)S(1)}, u32[]{:S(2)}, u32[]{:S(2)}) collective-permute-start(bf16[2048,512]{1,0:T(8,128)(2,1)} %bitcast.x_ref), channel_id=1, source_target_pairs={{0,1},{1,0},{2,3},{3,2},{4,5},{5,4},{6,7},{7,6},{8,9},{9,8},{10,11... | collective-permute-start | bytes 6291464 | tf_op jit(solution)/shard_map/ppermute | solution.py:39
  51.2 0.0 copy-done
  51.2 1.9 %collective-permute-start.2 = (s32[64]{0:T(128)S(1)}, s32[64]{0:T(128)S(1)}, u32[]{:S(2)}, u32[]{:S(2)}) collective-permute-start(s32[64]{0:T(128)S(1)} %copy-done), channel_id=1, source_target_pairs={{0,1},{1,0},{2,3},{3,2},{4,5},{5,4},{6,7},{7,6},{8,9},{9,8},{10,11... | collective-permute-start | bytes 776 | tf_op jit(solution)/shard_map/ppermute | solution.py:39
  53.1 1.8 %collective-permute-done.2 = s32[64]{0:T(128)S(1)} collective-permute-done((s32[64]{0:T(128)S(1)}, s32[64]{0:T(128)S(1)}, u32[]{:S(2)}, u32[]{:S(2)}) %collective-permute-start.2) | collective-permute-done | bytes 288 | tf_op jit(solution)/shard_map/ppermute | solution.py:39
  54.9 0.1 fusion
  55.0 0.1 collective-permute-done.1.y_ref
  55.1 6.4 %block_stats.1 = f32[2,1,1024]{2,1,0:T(1,128)S(1)} custom-call(bf16[2048,512]{1,0:T(8,128)(2,1)} %bitcast.x_ref, bf16[2048,512]{1,0:T(8,128)(2,1)S(1)} %collective-permute-done.1.y_ref), custom_call_target="tpu_custom_call" | custom-call | tf_op jit(solution)/shard_map/block_stats/pallas_call | solution.py:71
  61.6 14.3 %all_to_all.16 = f32[16,17,128]{2,1,0:T(8,128)S(1)} all-to-all(f32[16,17,128]{2,1,0:T(8,128)S(1)} %broadcast_in_dim.5), channel_id=1, replica_groups={{1,3,5,7,9,11,13,15,17,19,21,23,25,27,29,31},{33,35,37,39,41,43,45,47,4..., dimensions={0} | all-to-all | bytes 278528 | tf_op jit(solution)/shard_map/all_to_all | solution.py:43
  76.1 2.3 %collective-permute-start.3 = (f32[32,128]{1,0:T(8,128)S(1)}, f32[32,128]{1,0:T(8,128)S(1)}, u32[]{:S(2)}, u32[]{:S(2)}) collective-permute-start(f32[32,128]{1,0:T(8,128)S(1)} %pad_maximum_fusion), channel_id=1, source_target_pairs={{0,1},{1,0},{2,3},{3,2},{4,5},{5,4},{6,7},{7,6},{8,9},{9,8},{10,11... | collective-permute-start | bytes 49160 | tf_op jit(solution)/shard_map/ppermute | solution.py:39
  78.4 6.1 %block_scores.1.s_ref = f32[2048,2048]{1,0:T(8,128)S(1)} custom-call(bf16[2048,512]{1,0:T(8,128)(2,1)} %bitcast.x_ref, bf16[2048,512]{1,0:T(8,128)(2,1)S(1)} %collective-permute-done.1.y_ref), custom_call_target="tpu_custom_call" | custom-call | flops 4294967296 | bytes 20971520 | tf_op jit(solution)/shard_map/block_scores/pallas_call | solution.py:106
  84.5 0.0 collective-permute-done.3
  84.6 5.7 %block_grads.1 = bf16[2048,512]{1,0:T(8,128)(2,1)S(1)} custom-call(f32[2048,2048]{1,0:T(8,128)S(1)} %block_scores.1.s_ref, bf16[2048,512]{1,0:T(8,128)(2,1)S(1)} %collective-permute-done.1.y_ref, f32[16,128]{1,0:T(8,128)S(1)} %multiply_add_fusion.lx_ref, f32[16,128]{1,0:T(8,128)S(1)} %bitcast.10, f32[16,128]{1,0:T(8,128)S(1)} %get-tuple-element.5.ly_ref, ...), custom_call_target="tpu_custom_call" | custom-call | tf_op jit(solution)/shard_map/block_grads/pallas_call | solution.py:141
  90.2 34.0 %all_to_all.17 = bf16[16,128,512]{2,1,0:T(8,128)(2,1)S(1)} all-to-all(bf16[16,128,512]{2,1,0:T(8,128)(2,1)S(1)} %bitcast.8), channel_id=1, replica_groups={{1,3,5,7,9,11,13,15,17,19,21,23,25,27,29,31},{33,35,37,39,41,43,45,47,4..., dimensions={0} | all-to-all | bytes 4194304 | tf_op jit(solution)/shard_map/all_to_all | solution.py:43
  124.2 0.3 reduce_sum.22
  124.5 2.3 %collective-permute-start.4 = (bf16[128,512]{1,0:T(8,128)(2,1)S(1)}, bf16[128,512]{1,0:T(8,128)(2,1)S(1)}, u32[]{:S(2)}, u32[]{:S(2)}) collective-permute-start(bf16[128,512]{1,0:T(8,128)(2,1)S(1)} %reduce_sum.22), channel_id=1, source_target_pairs={{0,1},{1,0},{2,3},{3,2},{4,5},{5,4},{6,7},{7,6},{8,9},{9,8},{10,11... | collective-permute-start | bytes 393224 | tf_op jit(solution)/shard_map/ppermute | solution.py:39
  126.8 1.0 collective-permute-done.4
  127.8 0.7 slice_select_fusion
  (8 shorter events, 0.1 us)
Async XLA Ops:
  1.5 9.7 %collective-permute-start = (bf16[64,512]{1,0:T(8,128)(2,1)S(1)}, bf16[64,512]{1,0:T(8,128)(2,1)S(1)}, u32[]{:S(2)}, u32[]{:S(2)}) collective-permute-start(bf16[64,512]{1,0:T(8,128)(2,1)S(1)} %broadcast_select_fusion), channel_id=1, source_target_pairs={{0,1},{1,0},{2,3},{3,2},{4,5},{5,4},{6,7},{7,6},{8,9},{9,8},{10,11... | collective-permute-start | bytes 196616 | tf_op jit(solution)/shard_map/ppermute | solution.py:39
  12.3 38.9 %copy-start = (s32[64]{0:T(128)S(1)}, s32[64]{0:T(128)}, u32[]{:S(2)}) copy-start(s32[64]{0:T(128)} %param.5) | copy-start | bytes 772
  43.0 12.2 %collective-permute-start.1 = (bf16[2048,512]{1,0:T(8,128)(2,1)}, bf16[2048,512]{1,0:T(8,128)(2,1)S(1)}, u32[]{:S(2)}, u32[]{:S(2)}) collective-permute-start(bf16[2048,512]{1,0:T(8,128)(2,1)} %bitcast.x_ref), channel_id=1, source_target_pairs={{0,1},{1,0},{2,3},{3,2},{4,5},{5,4},{6,7},{7,6},{8,9},{9,8},{10,11... | collective-permute-start | bytes 6291464 | tf_op jit(solution)/shard_map/ppermute | solution.py:39
  51.2 3.8 %collective-permute-start.2 = (s32[64]{0:T(128)S(1)}, s32[64]{0:T(128)S(1)}, u32[]{:S(2)}, u32[]{:S(2)}) collective-permute-start(s32[64]{0:T(128)S(1)} %copy-done), channel_id=1, source_target_pairs={{0,1},{1,0},{2,3},{3,2},{4,5},{5,4},{6,7},{7,6},{8,9},{9,8},{10,11... | collective-permute-start | bytes 776 | tf_op jit(solution)/shard_map/ppermute | solution.py:39
  76.1 8.5 %collective-permute-start.3 = (f32[32,128]{1,0:T(8,128)S(1)}, f32[32,128]{1,0:T(8,128)S(1)}, u32[]{:S(2)}, u32[]{:S(2)}) collective-permute-start(f32[32,128]{1,0:T(8,128)S(1)} %pad_maximum_fusion), channel_id=1, source_target_pairs={{0,1},{1,0},{2,3},{3,2},{4,5},{5,4},{6,7},{7,6},{8,9},{9,8},{10,11... | collective-permute-start | bytes 49160 | tf_op jit(solution)/shard_map/ppermute | solution.py:39
  124.5 3.3 %collective-permute-start.4 = (bf16[128,512]{1,0:T(8,128)(2,1)S(1)}, bf16[128,512]{1,0:T(8,128)(2,1)S(1)}, u32[]{:S(2)}, u32[]{:S(2)}) collective-permute-start(bf16[128,512]{1,0:T(8,128)(2,1)S(1)} %reduce_sum.22), channel_id=1, source_target_pairs={{0,1},{1,0},{2,3},{3,2},{4,5},{5,4},{6,7},{7,6},{8,9},{9,8},{10,11... | collective-permute-start | bytes 393224 | tf_op jit(solution)/shard_map/ppermute | solution.py:39

commit v5 on v4

v5 whole, which is shorter than its diff:
```python
import functools
import math

import jax
import jax.numpy as jnp
from jax import lax
from jax.experimental import pallas as pl
from jax.experimental.pallas import tpu as pltpu
from jax.sharding import Mesh, PartitionSpec as P

TAU = 0.1
SCALE = math.log2(math.e) / TAU
AX = "d"
NZ, NX, NY, NC = 8, 4, 8, 2
DEVICES = NZ * NX * NY * NC
G = 16
LANES = 128


def dev(z, x, y, c):
    return ((z * NX + x) * NY + y) * NC + c


MOTION_GROUPS = [
    [dev(z, x, y, 1) for x in pair for y in range(NY)]
    for z in range(NZ)
    for pair in ((0, 1), (2, 3))
]
TEXT_GROUPS = [
    [dev(z, x, y, 0) for x in pair for z in range(NZ)]
    for y in range(NY)
    for pair in ((0, 3), (1, 2))
]
GROUPS = MOTION_GROUPS + TEXT_GROUPS
CORES = [(i, i ^ 1) for i in range(DEVICES)]


def swap(x):
    return lax.ppermute(x, AX, CORES)


def exchange(x):
    return lax.all_to_all(x, AX, 0, 0, axis_index_groups=GROUPS)


def spread(x):
    return exchange(jnp.broadcast_to(x[None], (G, *x.shape)))


def dot(a, b, dims):
    return lax.dot_general(a, b, (dims, ((), ())), preferred_element_type=jnp.float32)


VMEM = pl.BlockSpec(memory_space=pltpu.VMEM)


def stats_kernel(chunks, x_ref, y_ref, out_ref, s_ref):
    x = x_ref[...]
    block = x.shape[0]
    rows = pl.ds(pl.multiple_of(pl.program_id(0) * block, block), block)
    n = y_ref.shape[0] // chunks
    peaks, sums = [], []
    for c in range(chunks):
        s = dot(x, y_ref[c * n : (c + 1) * n, :], ((1,), (1,))) * SCALE
        s_ref[rows, c * n : (c + 1) * n] = s
        peak = jnp.max(s, axis=1, keepdims=True)
        peaks.append(peak)
        sums.append(jnp.sum(jnp.exp2(s - peak), axis=1, keepdims=True))
    peak = functools.reduce(jnp.maximum, peaks)
    total = sum(jnp.exp2(a - peak) * b for a, b in zip(peaks, sums))
    v = peak + jnp.log2(total)
    for r in range(block // LANES):
        column = v[r * LANES : (r + 1) * LANES]
        out_ref[0, r : r + 1, :] = jnp.transpose(jnp.broadcast_to(column, (LANES, LANES)))[:1]


def block_stats(x, y, block=512, chunks=4):
    rows, width = x.shape
    steps = rows // block
    out, scores = pl.pallas_call(
        functools.partial(stats_kernel, chunks),
        grid=(steps,),
        in_specs=[pl.BlockSpec((block, width), lambda i: (i, 0)), VMEM],
        out_specs=[pl.BlockSpec((1, block // LANES, LANES), lambda i: (i, 0, 0)), VMEM],
        out_shape=[
            jax.ShapeDtypeStruct((steps, block // LANES, LANES), jnp.float32),
            pltpu.VMEM((rows, y.shape[0]), jnp.float32),
        ],
        compiler_params=pltpu.CompilerParams(vmem_limit_bytes=20 << 20),
        name="block_stats",
    )(x, y)
    return out.reshape(rows // LANES, LANES), scores


def combine_kernel(stats_ref, out_ref):
    parts = stats_ref[:, :G, :]
    peak = jnp.max(parts, axis=0)
    out_ref[:G, :] = peak + jnp.log2(jnp.sum(jnp.exp2(parts - peak), axis=0))
    out_ref[G:, :] = jnp.concatenate([stats_ref[g, G:, :] for g in range(G)])


def combine(stats):
    return pl.pallas_call(
        combine_kernel,
        in_specs=[VMEM],
        out_specs=VMEM,
        out_shape=jax.ShapeDtypeStruct((2 * G, LANES), jnp.float32),
        compiler_params=pltpu.CompilerParams(vmem_limit_bytes=4 << 20),
        name="combine",
    )(stats)


def columns(ref, first, count):
    return jnp.concatenate(
        [
            jnp.transpose(jnp.broadcast_to(ref[pl.ds(first + r, 1), :], (LANES, LANES)))
            for r in range(count)
        ]
    )


def grads_kernel(s_ref, y_ref, own_ref, other_ref, out_ref):
    block = out_ref.shape[0]
    count = block // LANES
    step = pl.program_id(0)
    lx = columns(own_ref, step * count, count)
    kx = columns(own_ref, G + step * count, count)
    rows = pl.ds(pl.multiple_of(step * block, block), block)
    weights = []
    for r in range(s_ref.shape[1] // LANES):
        s = s_ref[rows, r * LANES : (r + 1) * LANES]
        w = jnp.exp2(s - lx) + jnp.exp2(s - other_ref[r : r + 1, :])
        w = jnp.where(kx == other_ref[G + r : G + r + 1, :], w - 2.0, w) * (0.5 / TAU)
        weights.append(w.astype(jnp.bfloat16))
    w = jnp.concatenate(weights, axis=1)
    out_ref[...] = dot(w, y_ref[...], ((1,), (0,))).astype(jnp.bfloat16)


def block_grads(scores, y, own, other, block=1024):
    rows = scores.shape[0]
    width = y.shape[1]
    return pl.pallas_call(
        grads_kernel,
        grid=(rows // block,),
        in_specs=[VMEM, VMEM, VMEM, VMEM],
        out_specs=pl.BlockSpec((block, width), lambda i: (i, 0)),
        out_shape=jax.ShapeDtypeStruct((rows, width), jnp.bfloat16),
        compiler_params=pltpu.CompilerParams(vmem_limit_bytes=28 << 20),
        name="block_grads",
    )(scores, y, own, other)


def per_device(motion, text, pair_text):
    n, width = motion.shape
    d = lax.axis_index(AX)
    is_text = d % NC == 0
    got = swap(jnp.where(is_text, motion, text))
    mine = jnp.where(is_text, jnp.concatenate([text, got]), jnp.concatenate([got, motion]))
    x = spread(mine).reshape(G * NC * n, width)
    y = swap(x)
    pair_got = swap(pair_text)
    ids = d // NC * (NC * n) + lax.iota(jnp.int32, NC * n)
    key = jnp.where(is_text, ids, jnp.concatenate([pair_got, pair_text])).astype(jnp.float32)
    part, scores = block_stats(x, y)
    own = combine(spread(jnp.concatenate([part, key[None]])))
    grad_part = block_grads(scores, y, own, swap(own))
    grads = exchange(grad_part.reshape(G, NC * n, width))
    grad = jnp.sum(grads.astype(jnp.float32), axis=0).astype(jnp.bfloat16)
    grad_got = swap(grad)
    motion_grad = jnp.where(is_text, grad_got[:n], grad[n:])
    text_grad = jnp.where(is_text, grad[:n], grad_got[n:])
    return (motion_grad, text_grad)


def solution(mesh):
    flat = Mesh(mesh.devices.reshape(DEVICES), (AX,))
    return jax.shard_map(
        per_device,
        mesh=flat,
        in_specs=(P(AX, None), P(AX, None), P(AX)),
        out_specs=(P(AX, None), P(AX, None)),
        check_vma=False,
    )
```

time: 129 us -> 125 us (0.969)
  Pallas kernels: 18.2 us -> 13.3 us
    pallas_call x1, Pallas kernels: 6.15 us -> 0.04 us  [combine(): pl.pallas_call(combine_kernel, in_specs=[VMEM], out_specs=VMEM, out_shape...]
  transfers between devices with their start and end apart: 5 -> 5, of which waited for: 4 -> 5; matrix products, arithmetic and copies ran while one was open for 0% -> 0% of each run, Pallas kernels for 5% -> 0%
where the time goes in v5:
time: 125 us; the launch traced here: 124 us
  blocking collectives  79 us (63%)
  starting transfers between devices  23.5 us (19%)
  Pallas kernels  13.3 us (11%)
  waiting for transfers between devices  4.61 us (4%)
  other arithmetic  2.81 us (2%)
    all_to_all x3, blocking collectives, exchange(): return lax.all_to_all(x, AX, 0, 0, axis_index_groups=GROUPS)  79 us
    ppermute x5, starting transfers between devices, swap(): return lax.ppermute(x, AX, CORES)  23.5 us
    pallas_call x1, Pallas kernels, block_stats(): pl.pallas_call(functools.partial(stats_kernel, chunks), grid=(steps,), in...  7.63 us
    pallas_call x1, Pallas kernels, block_grads(): pl.pallas_call(grads_kernel, grid=(rows // block,), in_specs=[VMEM, VMEM,...  5.61 us
    ppermute x5, waiting for transfers between devices, swap(): return lax.ppermute(x, AX, CORES)  4.61 us
  transfers between devices with their start and end apart: 5, of which 5 were waited for; matrix products, arithmetic and copies ran while one was open for 0% of the time, Pallas kernels for 0%

profile of v5, /device:TPU:1, one launch (start us, length us, event | category | flops | bytes accessed | tf_op | source)
XLA Modules:
  0.0 124.2 jit_solution(11914236114265367438)
XLA Ops:
  0.6 0.9 broadcast_select_fusion
  1.5 8.8 %collective-permute-start = (bf16[64,512]{1,0:T(8,128)(2,1)S(1)}, bf16[64,512]{1,0:T(8,128)(2,1)S(1)}, u32[]{:S(2)}, u32[]{:S(2)}) collective-permute-start(bf16[64,512]{1,0:T(8,128)(2,1)S(1)} %broadcast_select_fusion), channel_id=1, source_target_pairs={{0,1},{1,0},{2,3},{3,2},{4,5},{5,4},{6,7},{7,6},{8,9},{9,8},{10,11... | collective-permute-start | bytes 196616 | tf_op jit(solution)/shard_map/ppermute | solution.py:39
  10.3 0.9 collective-permute-done
  11.2 0.9 maximum_select_fusion
  12.1 0.2 broadcast_in_dim.4
  12.3 0.0 copy-start
  12.3 30.7 %all_to_all.15 = bf16[16,128,512]{2,1,0:T(8,128)(2,1)} all-to-all(bf16[16,128,512]{2,1,0:T(8,128)(2,1)S(1)} %broadcast_in_dim.4), channel_id=1, replica_groups={{1,3,5,7,9,11,13,15,17,19,21,23,25,27,29,31},{33,35,37,39,41,43,45,47,4..., dimensions={0} | all-to-all | bytes 4194304 | tf_op jit(solution)/shard_map/all_to_all | solution.py:43
  43.0 8.2 %collective-permute-start.1 = (bf16[2048,512]{1,0:T(8,128)(2,1)}, bf16[2048,512]{1,0:T(8,128)(2,1)S(1)}, u32[]{:S(2)}, u32[]{:S(2)}) collective-permute-start(bf16[2048,512]{1,0:T(8,128)(2,1)} %bitcast.x_ref), channel_id=1, source_target_pairs={{0,1},{1,0},{2,3},{3,2},{4,5},{5,4},{6,7},{7,6},{8,9},{9,8},{10,11... | collective-permute-start | bytes 6291464 | tf_op jit(solution)/shard_map/ppermute | solution.py:39
  51.2 0.0 copy-done
  51.2 1.9 %collective-permute-start.2 = (s32[64]{0:T(128)S(1)}, s32[64]{0:T(128)S(1)}, u32[]{:S(2)}, u32[]{:S(2)}) collective-permute-start(s32[64]{0:T(128)S(1)} %copy-done), channel_id=1, source_target_pairs={{0,1},{1,0},{2,3},{3,2},{4,5},{5,4},{6,7},{7,6},{8,9},{9,8},{10,11... | collective-permute-start | bytes 776 | tf_op jit(solution)/shard_map/ppermute | solution.py:39
  53.1 1.8 %collective-permute-done.2 = s32[64]{0:T(128)S(1)} collective-permute-done((s32[64]{0:T(128)S(1)}, s32[64]{0:T(128)S(1)}, u32[]{:S(2)}, u32[]{:S(2)}) %collective-permute-start.2) | collective-permute-done | bytes 288 | tf_op jit(solution)/shard_map/ppermute | solution.py:39
  54.9 0.1 fusion
  55.0 0.1 collective-permute-done.1.y_ref
  55.1 7.6 %block_stats.1 = (f32[4,4,128]{2,1,0:T(4,128)S(1)}, f32[2048,2048]{1,0:T(8,128)S(1)}) custom-call(bf16[2048,512]{1,0:T(8,128)(2,1)} %bitcast.x_ref, bf16[2048,512]{1,0:T(8,128)(2,1)S(1)} %collective-permute-done.1.y_ref), custom_call_target="tpu_custom_call" | custom-call | tf_op jit(solution)/shard_map/block_stats/pallas_call | solution.py:80
  62.8 14.3 %all_to_all.16.stats_ref = f32[16,17,128]{2,1,0:T(8,128)S(1)} all-to-all(f32[16,17,128]{2,1,0:T(8,128)S(1)} %broadcast_in_dim.5), channel_id=1, replica_groups={{1,3,5,7,9,11,13,15,17,19,21,23,25,27,29,31},{33,35,37,39,41,43,45,47,4..., dimensions={0} | all-to-all | bytes 278528 | tf_op jit(solution)/shard_map/all_to_all | solution.py:43
  77.2 2.3 %collective-permute-start.3 = (f32[32,128]{1,0:T(8,128)S(1)}, f32[32,128]{1,0:T(8,128)S(1)}, u32[]{:S(2)}, u32[]{:S(2)}) collective-permute-start(f32[32,128]{1,0:T(8,128)S(1)} %combine.1.own_ref), channel_id=1, source_target_pairs={{0,1},{1,0},{2,3},{3,2},{4,5},{5,4},{6,7},{7,6},{8,9},{9,8},{10,11... | collective-permute-start | bytes 49160 | tf_op jit(solution)/shard_map/ppermute | solution.py:39
  79.5 0.8 collective-permute-done.3.other_ref
  80.3 5.6 %block_grads.1 = bf16[2048,512]{1,0:T(8,128)(2,1)S(1)} custom-call(f32[2048,2048]{1,0:T(8,128)S(1)} %get-tuple-element.4.s_ref, bf16[2048,512]{1,0:T(8,128)(2,1)S(1)} %collective-permute-done.1.y_ref, f32[32,128]{1,0:T(8,128)S(1)} %combine.1.own_ref, f32[32,128]{1,0:T(8,128)S(1)} %collective-permute-done.3.other_ref), custom_call_target="tpu_custom_call" | custom-call | tf_op jit(solution)/shard_map/block_grads/pallas_call | solution.py:142
  86.0 34.0 %all_to_all.17 = bf16[16,128,512]{2,1,0:T(8,128)(2,1)S(1)} all-to-all(bf16[16,128,512]{2,1,0:T(8,128)(2,1)S(1)} %bitcast.5), channel_id=1, replica_groups={{1,3,5,7,9,11,13,15,17,19,21,23,25,27,29,31},{33,35,37,39,41,43,45,47,4..., dimensions={0} | all-to-all | bytes 4194304 | tf_op jit(solution)/shard_map/all_to_all | solution.py:43
  119.9 0.3 reduce_sum.12
  120.2 2.3 %collective-permute-start.4 = (bf16[128,512]{1,0:T(8,128)(2,1)S(1)}, bf16[128,512]{1,0:T(8,128)(2,1)S(1)}, u32[]{:S(2)}, u32[]{:S(2)}) collective-permute-start(bf16[128,512]{1,0:T(8,128)(2,1)S(1)} %reduce_sum.12), channel_id=1, source_target_pairs={{0,1},{1,0},{2,3},{3,2},{4,5},{5,4},{6,7},{7,6},{8,9},{9,8},{10,11... | collective-permute-start | bytes 393224 | tf_op jit(solution)/shard_map/ppermute | solution.py:39
  122.6 1.0 collective-permute-done.4
  123.5 0.7 slice_select_fusion
  (3 shorter events, 0.1 us)
Async XLA Ops:
  1.5 9.7 %collective-permute-start = (bf16[64,512]{1,0:T(8,128)(2,1)S(1)}, bf16[64,512]{1,0:T(8,128)(2,1)S(1)}, u32[]{:S(2)}, u32[]{:S(2)}) collective-permute-start(bf16[64,512]{1,0:T(8,128)(2,1)S(1)} %broadcast_select_fusion), channel_id=1, source_target_pairs={{0,1},{1,0},{2,3},{3,2},{4,5},{5,4},{6,7},{7,6},{8,9},{9,8},{10,11... | collective-permute-start | bytes 196616 | tf_op jit(solution)/shard_map/ppermute | solution.py:39
  12.3 38.9 %copy-start = (s32[64]{0:T(128)S(1)}, s32[64]{0:T(128)}, u32[]{:S(2)}) copy-start(s32[64]{0:T(128)} %param.5) | copy-start | bytes 772
  43.0 12.2 %collective-permute-start.1 = (bf16[2048,512]{1,0:T(8,128)(2,1)}, bf16[2048,512]{1,0:T(8,128)(2,1)S(1)}, u32[]{:S(2)}, u32[]{:S(2)}) collective-permute-start(bf16[2048,512]{1,0:T(8,128)(2,1)} %bitcast.x_ref), channel_id=1, source_target_pairs={{0,1},{1,0},{2,3},{3,2},{4,5},{5,4},{6,7},{7,6},{8,9},{9,8},{10,11... | collective-permute-start | bytes 6291464 | tf_op jit(solution)/shard_map/ppermute | solution.py:39
  51.2 3.8 %collective-permute-start.2 = (s32[64]{0:T(128)S(1)}, s32[64]{0:T(128)S(1)}, u32[]{:S(2)}, u32[]{:S(2)}) collective-permute-start(s32[64]{0:T(128)S(1)} %copy-done), channel_id=1, source_target_pairs={{0,1},{1,0},{2,3},{3,2},{4,5},{5,4},{6,7},{7,6},{8,9},{9,8},{10,11... | collective-permute-start | bytes 776 | tf_op jit(solution)/shard_map/ppermute | solution.py:39
  77.2 3.1 %collective-permute-start.3 = (f32[32,128]{1,0:T(8,128)S(1)}, f32[32,128]{1,0:T(8,128)S(1)}, u32[]{:S(2)}, u32[]{:S(2)}) collective-permute-start(f32[32,128]{1,0:T(8,128)S(1)} %combine.1.own_ref), channel_id=1, source_target_pairs={{0,1},{1,0},{2,3},{3,2},{4,5},{5,4},{6,7},{7,6},{8,9},{9,8},{10,11... | collective-permute-start | bytes 49160 | tf_op jit(solution)/shard_map/ppermute | solution.py:39
  120.2 3.3 %collective-permute-start.4 = (bf16[128,512]{1,0:T(8,128)(2,1)S(1)}, bf16[128,512]{1,0:T(8,128)(2,1)S(1)}, u32[]{:S(2)}, u32[]{:S(2)}) collective-permute-start(bf16[128,512]{1,0:T(8,128)(2,1)S(1)} %reduce_sum.12), channel_id=1, source_target_pairs={{0,1},{1,0},{2,3},{3,2},{4,5},{5,4},{6,7},{7,6},{8,9},{9,8},{10,11... | collective-permute-start | bytes 393224 | tf_op jit(solution)/shard_map/ppermute | solution.py:39

commit v6 on v5

--- a/solution.py
+++ b/solution.py
@@ -10,6 +10,7 @@
 
 TAU = 0.1
 SCALE = math.log2(math.e) / TAU
+FACTOR = math.log2(0.5 / TAU)
 AX = "d"
 NZ, NX, NY, NC = 8, 4, 8, 2
 DEVICES = NZ * NX * NY * NC
@@ -95,7 +96,7 @@
 def combine_kernel(stats_ref, out_ref):
     parts = stats_ref[:, :G, :]
     peak = jnp.max(parts, axis=0)
-    out_ref[:G, :] = peak + jnp.log2(jnp.sum(jnp.exp2(parts - peak), axis=0))
+    out_ref[:G, :] = (peak - FACTOR) + jnp.log2(jnp.sum(jnp.exp2(parts - peak), axis=0))
     out_ref[G:, :] = jnp.concatenate([stats_ref[g, G:, :] for g in range(G)])
 
 
@@ -130,7 +131,7 @@
     for r in range(s_ref.shape[1] // LANES):
         s = s_ref[rows, r * LANES : (r + 1) * LANES]
         w = jnp.exp2(s - lx) + jnp.exp2(s - other_ref[r : r + 1, :])
-        w = jnp.where(kx == other_ref[G + r : G + r + 1, :], w - 2.0, w) * (0.5 / TAU)
+        w = jnp.where(kx == other_ref[G + r : G + r + 1, :], w - 1.0 / TAU, w)
         weights.append(w.astype(jnp.bfloat16))
     w = jnp.concatenate(weights, axis=1)
     out_ref[...] = dot(w, y_ref[...], ((1,), (0,))).astype(jnp.bfloat16)

time: 125 us -> 124 us (level)
  no operation moved by 1% of the time
where the time goes in v6:
time: 124 us
  blocking collectives  79 us (64%)
  starting transfers between devices  23.5 us (19%)
  Pallas kernels  12.8 us (10%)
  waiting for transfers between devices  4.61 us (4%)
  other arithmetic  2.81 us (2%)
    all_to_all x3, blocking collectives, exchange(): return lax.all_to_all(x, AX, 0, 0, axis_index_groups=GROUPS)  79 us
    ppermute x5, starting transfers between devices, swap(): return lax.ppermute(x, AX, CORES)  23.5 us
    pallas_call x1, Pallas kernels, block_stats(): pl.pallas_call(functools.partial(stats_kernel, chunks), grid=(steps,), in...  7.63 us
    pallas_call x1, Pallas kernels, block_grads(): pl.pallas_call(grads_kernel, grid=(rows // block,), in_specs=[VMEM, VMEM,...  5.16 us
    ppermute x5, waiting for transfers between devices, swap(): return lax.ppermute(x, AX, CORES)  4.61 us
  transfers between devices with their start and end apart: 5, of which 5 were waited for; matrix products, arithmetic and copies ran while one was open for 0% of the time, Pallas kernels for 0%

profile of v6, /device:TPU:1, one launch (start us, length us, event | category | flops | bytes accessed | tf_op | source)
XLA Modules:
  0.0 123.7 jit_solution(3991557584079885117)
XLA Ops:
  0.6 0.9 broadcast_select_fusion
  1.5 8.8 %collective-permute-start = (bf16[64,512]{1,0:T(8,128)(2,1)S(1)}, bf16[64,512]{1,0:T(8,128)(2,1)S(1)}, u32[]{:S(2)}, u32[]{:S(2)}) collective-permute-start(bf16[64,512]{1,0:T(8,128)(2,1)S(1)} %broadcast_select_fusion), channel_id=1, source_target_pairs={{0,1},{1,0},{2,3},{3,2},{4,5},{5,4},{6,7},{7,6},{8,9},{9,8},{10,11... | collective-permute-start | bytes 196616 | tf_op jit(solution)/shard_map/ppermute | solution.py:40
  10.3 0.9 collective-permute-done
  11.2 0.9 maximum_select_fusion
  12.1 0.2 broadcast_in_dim.4
  12.3 0.0 copy-start
  12.3 30.7 %all_to_all.15 = bf16[16,128,512]{2,1,0:T(8,128)(2,1)} all-to-all(bf16[16,128,512]{2,1,0:T(8,128)(2,1)S(1)} %broadcast_in_dim.4), channel_id=1, replica_groups={{1,3,5,7,9,11,13,15,17,19,21,23,25,27,29,31},{33,35,37,39,41,43,45,47,4..., dimensions={0} | all-to-all | bytes 4194304 | tf_op jit(solution)/shard_map/all_to_all | solution.py:44
  43.0 8.2 %collective-permute-start.1 = (bf16[2048,512]{1,0:T(8,128)(2,1)}, bf16[2048,512]{1,0:T(8,128)(2,1)S(1)}, u32[]{:S(2)}, u32[]{:S(2)}) collective-permute-start(bf16[2048,512]{1,0:T(8,128)(2,1)} %bitcast.x_ref), channel_id=1, source_target_pairs={{0,1},{1,0},{2,3},{3,2},{4,5},{5,4},{6,7},{7,6},{8,9},{9,8},{10,11... | collective-permute-start | bytes 6291464 | tf_op jit(solution)/shard_map/ppermute | solution.py:40
  51.2 0.0 copy-done
  51.2 1.9 %collective-permute-start.2 = (s32[64]{0:T(128)S(1)}, s32[64]{0:T(128)S(1)}, u32[]{:S(2)}, u32[]{:S(2)}) collective-permute-start(s32[64]{0:T(128)S(1)} %copy-done), channel_id=1, source_target_pairs={{0,1},{1,0},{2,3},{3,2},{4,5},{5,4},{6,7},{7,6},{8,9},{9,8},{10,11... | collective-permute-start | bytes 776 | tf_op jit(solution)/shard_map/ppermute | solution.py:40
  53.1 1.8 %collective-permute-done.2 = s32[64]{0:T(128)S(1)} collective-permute-done((s32[64]{0:T(128)S(1)}, s32[64]{0:T(128)S(1)}, u32[]{:S(2)}, u32[]{:S(2)}) %collective-permute-start.2) | collective-permute-done | bytes 288 | tf_op jit(solution)/shard_map/ppermute | solution.py:40
  54.9 0.1 fusion
  55.0 0.1 collective-permute-done.1.y_ref
  55.1 7.6 %block_stats.1 = (f32[4,4,128]{2,1,0:T(4,128)S(1)}, f32[2048,2048]{1,0:T(8,128)S(1)}) custom-call(bf16[2048,512]{1,0:T(8,128)(2,1)} %bitcast.x_ref, bf16[2048,512]{1,0:T(8,128)(2,1)S(1)} %collective-permute-done.1.y_ref), custom_call_target="tpu_custom_call" | custom-call | tf_op jit(solution)/shard_map/block_stats/pallas_call | solution.py:81
  62.8 14.3 %all_to_all.16.stats_ref = f32[16,17,128]{2,1,0:T(8,128)S(1)} all-to-all(f32[16,17,128]{2,1,0:T(8,128)S(1)} %broadcast_in_dim.5), channel_id=1, replica_groups={{1,3,5,7,9,11,13,15,17,19,21,23,25,27,29,31},{33,35,37,39,41,43,45,47,4..., dimensions={0} | all-to-all | bytes 278528 | tf_op jit(solution)/shard_map/all_to_all | solution.py:44
  77.2 2.3 %collective-permute-start.3 = (f32[32,128]{1,0:T(8,128)S(1)}, f32[32,128]{1,0:T(8,128)S(1)}, u32[]{:S(2)}, u32[]{:S(2)}) collective-permute-start(f32[32,128]{1,0:T(8,128)S(1)} %combine.1.own_ref), channel_id=1, source_target_pairs={{0,1},{1,0},{2,3},{3,2},{4,5},{5,4},{6,7},{7,6},{8,9},{9,8},{10,11... | collective-permute-start | bytes 49160 | tf_op jit(solution)/shard_map/ppermute | solution.py:40
  79.5 0.8 collective-permute-done.3.other_ref
  80.3 5.2 %block_grads.1 = bf16[2048,512]{1,0:T(8,128)(2,1)S(1)} custom-call(f32[2048,2048]{1,0:T(8,128)S(1)} %get-tuple-element.4.s_ref, bf16[2048,512]{1,0:T(8,128)(2,1)S(1)} %collective-permute-done.1.y_ref, f32[32,128]{1,0:T(8,128)S(1)} %combine.1.own_ref, f32[32,128]{1,0:T(8,128)S(1)} %collective-permute-done.3.other_ref), custom_call_target="tpu_custom_call" | custom-call | tf_op jit(solution)/shard_map/block_grads/pallas_call | solution.py:143
  85.5 34.0 %all_to_all.17 = bf16[16,128,512]{2,1,0:T(8,128)(2,1)S(1)} all-to-all(bf16[16,128,512]{2,1,0:T(8,128)(2,1)S(1)} %bitcast.5), channel_id=1, replica_groups={{1,3,5,7,9,11,13,15,17,19,21,23,25,27,29,31},{33,35,37,39,41,43,45,47,4..., dimensions={0} | all-to-all | bytes 4194304 | tf_op jit(solution)/shard_map/all_to_all | solution.py:44
  119.5 0.3 reduce_sum.12
  119.8 2.3 %collective-permute-start.4 = (bf16[128,512]{1,0:T(8,128)(2,1)S(1)}, bf16[128,512]{1,0:T(8,128)(2,1)S(1)}, u32[]{:S(2)}, u32[]{:S(2)}) collective-permute-start(bf16[128,512]{1,0:T(8,128)(2,1)S(1)} %reduce_sum.12), channel_id=1, source_target_pairs={{0,1},{1,0},{2,3},{3,2},{4,5},{5,4},{6,7},{7,6},{8,9},{9,8},{10,11... | collective-permute-start | bytes 393224 | tf_op jit(solution)/shard_map/ppermute | solution.py:40
  122.1 1.0 collective-permute-done.4
  123.1 0.7 slice_select_fusion
  (3 shorter events, 0.1 us)
Async XLA Ops:
  1.5 9.7 %collective-permute-start = (bf16[64,512]{1,0:T(8,128)(2,1)S(1)}, bf16[64,512]{1,0:T(8,128)(2,1)S(1)}, u32[]{:S(2)}, u32[]{:S(2)}) collective-permute-start(bf16[64,512]{1,0:T(8,128)(2,1)S(1)} %broadcast_select_fusion), channel_id=1, source_target_pairs={{0,1},{1,0},{2,3},{3,2},{4,5},{5,4},{6,7},{7,6},{8,9},{9,8},{10,11... | collective-permute-start | bytes 196616 | tf_op jit(solution)/shard_map/ppermute | solution.py:40
  12.3 38.9 %copy-start = (s32[64]{0:T(128)S(1)}, s32[64]{0:T(128)}, u32[]{:S(2)}) copy-start(s32[64]{0:T(128)} %param.5) | copy-start | bytes 772
  43.0 12.2 %collective-permute-start.1 = (bf16[2048,512]{1,0:T(8,128)(2,1)}, bf16[2048,512]{1,0:T(8,128)(2,1)S(1)}, u32[]{:S(2)}, u32[]{:S(2)}) collective-permute-start(bf16[2048,512]{1,0:T(8,128)(2,1)} %bitcast.x_ref), channel_id=1, source_target_pairs={{0,1},{1,0},{2,3},{3,2},{4,5},{5,4},{6,7},{7,6},{8,9},{9,8},{10,11... | collective-permute-start | bytes 6291464 | tf_op jit(solution)/shard_map/ppermute | solution.py:40
  51.2 3.8 %collective-permute-start.2 = (s32[64]{0:T(128)S(1)}, s32[64]{0:T(128)S(1)}, u32[]{:S(2)}, u32[]{:S(2)}) collective-permute-start(s32[64]{0:T(128)S(1)} %copy-done), channel_id=1, source_target_pairs={{0,1},{1,0},{2,3},{3,2},{4,5},{5,4},{6,7},{7,6},{8,9},{9,8},{10,11... | collective-permute-start | bytes 776 | tf_op jit(solution)/shard_map/ppermute | solution.py:40
  77.2 3.1 %collective-permute-start.3 = (f32[32,128]{1,0:T(8,128)S(1)}, f32[32,128]{1,0:T(8,128)S(1)}, u32[]{:S(2)}, u32[]{:S(2)}) collective-permute-start(f32[32,128]{1,0:T(8,128)S(1)} %combine.1.own_ref), channel_id=1, source_target_pairs={{0,1},{1,0},{2,3},{3,2},{4,5},{5,4},{6,7},{7,6},{8,9},{9,8},{10,11... | collective-permute-start | bytes 49160 | tf_op jit(solution)/shard_map/ppermute | solution.py:40
  119.8 3.3 %collective-permute-start.4 = (bf16[128,512]{1,0:T(8,128)(2,1)S(1)}, bf16[128,512]{1,0:T(8,128)(2,1)S(1)}, u32[]{:S(2)}, u32[]{:S(2)}) collective-permute-start(bf16[128,512]{1,0:T(8,128)(2,1)S(1)} %reduce_sum.12), channel_id=1, source_target_pairs={{0,1},{1,0},{2,3},{3,2},{4,5},{5,4},{6,7},{7,6},{8,9},{9,8},{10,11... | collective-permute-start | bytes 393224 | tf_op jit(solution)/shard_map/ppermute | solution.py:40

commit v7 on v6

--- a/solution.py
+++ b/solution.py
@@ -155,8 +155,9 @@
     n, width = motion.shape
     d = lax.axis_index(AX)
     is_text = d % NC == 0
+    shard = lax.optimization_barrier(jnp.where(is_text, text, motion))
     got = swap(jnp.where(is_text, motion, text))
-    mine = jnp.where(is_text, jnp.concatenate([text, got]), jnp.concatenate([got, motion]))
+    mine = jnp.where(is_text, jnp.concatenate([shard, got]), jnp.concatenate([got, shard]))
     x = spread(mine).reshape(G * NC * n, width)
     y = swap(x)
     pair_got = swap(pair_text)

time: 124 us -> 123 us (level)
  no operation moved by 1% of the time
where the time goes in v7:
time: 123 us
  blocking collectives  79 us (64%)
  starting transfers between devices  23.5 us (19%)
  Pallas kernels  12.8 us (10%)
  waiting for transfers between devices  4.61 us (4%)
  other arithmetic  1.95 us (2%)
    all_to_all x3, blocking collectives, exchange(): return lax.all_to_all(x, AX, 0, 0, axis_index_groups=GROUPS)  79 us
    ppermute x5, starting transfers between devices, swap(): return lax.ppermute(x, AX, CORES)  23.5 us
    pallas_call x1, Pallas kernels, block_stats(): pl.pallas_call(functools.partial(stats_kernel, chunks), grid=(steps,), in...  7.63 us
    pallas_call x1, Pallas kernels, block_grads(): pl.pallas_call(grads_kernel, grid=(rows // block,), in_specs=[VMEM, VMEM,...  5.16 us
    ppermute x5, waiting for transfers between devices, swap(): return lax.ppermute(x, AX, CORES)  4.61 us
  transfers between devices with their start and end apart: 5, of which 5 were waited for; matrix products, arithmetic and copies ran while one was open for 0% of the time, Pallas kernels for 0%

profile of v7, /device:TPU:1, one launch (start us, length us, event | category | flops | bytes accessed | tf_op | source)
XLA Modules:
  0.0 122.9 jit_solution(17588908294745965073)
XLA Ops:
  0.6 0.9 broadcast_select_fusion.1
  1.5 8.8 %collective-permute-start = (bf16[64,512]{1,0:T(8,128)(2,1)S(1)}, bf16[64,512]{1,0:T(8,128)(2,1)S(1)}, u32[]{:S(2)}, u32[]{:S(2)}) collective-permute-start(bf16[64,512]{1,0:T(8,128)(2,1)S(1)} %get-tuple-element.9), channel_id=1, source_target_pairs={{0,1},{1,0},{2,3},{3,2},{4,5},{5,4},{6,7},{7,6},{8,9},{9,8},{10,11... | collective-permute-start | bytes 196616 | tf_op jit(solution)/shard_map/ppermute | solution.py:40
  10.3 0.9 collective-permute-done
  11.2 0.2 broadcast_in_dim.4
  11.4 0.0 copy-start
  11.5 30.7 %all_to_all.15 = bf16[16,128,512]{2,1,0:T(8,128)(2,1)} all-to-all(bf16[16,128,512]{2,1,0:T(8,128)(2,1)S(1)} %broadcast_in_dim.4), channel_id=1, replica_groups={{1,3,5,7,9,11,13,15,17,19,21,23,25,27,29,31},{33,35,37,39,41,43,45,47,4..., dimensions={0} | all-to-all | bytes 4194304 | tf_op jit(solution)/shard_map/all_to_all | solution.py:44
  42.1 8.2 %collective-permute-start.1 = (bf16[2048,512]{1,0:T(8,128)(2,1)}, bf16[2048,512]{1,0:T(8,128)(2,1)S(1)}, u32[]{:S(2)}, u32[]{:S(2)}) collective-permute-start(bf16[2048,512]{1,0:T(8,128)(2,1)} %bitcast.x_ref), channel_id=1, source_target_pairs={{0,1},{1,0},{2,3},{3,2},{4,5},{5,4},{6,7},{7,6},{8,9},{9,8},{10,11... | collective-permute-start | bytes 6291464 | tf_op jit(solution)/shard_map/ppermute | solution.py:40
  50.3 0.0 copy-done
  50.3 1.9 %collective-permute-start.2 = (s32[64]{0:T(128)S(1)}, s32[64]{0:T(128)S(1)}, u32[]{:S(2)}, u32[]{:S(2)}) collective-permute-start(s32[64]{0:T(128)S(1)} %copy-done), channel_id=1, source_target_pairs={{0,1},{1,0},{2,3},{3,2},{4,5},{5,4},{6,7},{7,6},{8,9},{9,8},{10,11... | collective-permute-start | bytes 776 | tf_op jit(solution)/shard_map/ppermute | solution.py:40
  52.3 1.8 %collective-permute-done.2 = s32[64]{0:T(128)S(1)} collective-permute-done((s32[64]{0:T(128)S(1)}, s32[64]{0:T(128)S(1)}, u32[]{:S(2)}, u32[]{:S(2)}) %collective-permute-start.2) | collective-permute-done | bytes 288 | tf_op jit(solution)/shard_map/ppermute | solution.py:40
  54.1 0.1 fusion
  54.2 0.1 collective-permute-done.1.y_ref
  54.3 7.6 %block_stats.1 = (f32[4,4,128]{2,1,0:T(4,128)S(1)}, f32[2048,2048]{1,0:T(8,128)S(1)}) custom-call(bf16[2048,512]{1,0:T(8,128)(2,1)} %bitcast.x_ref, bf16[2048,512]{1,0:T(8,128)(2,1)S(1)} %collective-permute-done.1.y_ref), custom_call_target="tpu_custom_call" | custom-call | tf_op jit(solution)/shard_map/block_stats/pallas_call | solution.py:81
  62.0 14.4 %all_to_all.16.stats_ref = f32[16,17,128]{2,1,0:T(8,128)S(1)} all-to-all(f32[16,17,128]{2,1,0:T(8,128)S(1)} %broadcast_in_dim.5), channel_id=1, replica_groups={{1,3,5,7,9,11,13,15,17,19,21,23,25,27,29,31},{33,35,37,39,41,43,45,47,4..., dimensions={0} | all-to-all | bytes 278528 | tf_op jit(solution)/shard_map/all_to_all | solution.py:44
  76.4 2.3 %collective-permute-start.3 = (f32[32,128]{1,0:T(8,128)S(1)}, f32[32,128]{1,0:T(8,128)S(1)}, u32[]{:S(2)}, u32[]{:S(2)}) collective-permute-start(f32[32,128]{1,0:T(8,128)S(1)} %combine.1.own_ref), channel_id=1, source_target_pairs={{0,1},{1,0},{2,3},{3,2},{4,5},{5,4},{6,7},{7,6},{8,9},{9,8},{10,11... | collective-permute-start | bytes 49160 | tf_op jit(solution)/shard_map/ppermute | solution.py:40
  78.7 0.8 collective-permute-done.3.other_ref
  79.5 5.2 %block_grads.1 = bf16[2048,512]{1,0:T(8,128)(2,1)S(1)} custom-call(f32[2048,2048]{1,0:T(8,128)S(1)} %get-tuple-element.4.s_ref, bf16[2048,512]{1,0:T(8,128)(2,1)S(1)} %collective-permute-done.1.y_ref, f32[32,128]{1,0:T(8,128)S(1)} %combine.1.own_ref, f32[32,128]{1,0:T(8,128)S(1)} %collective-permute-done.3.other_ref), custom_call_target="tpu_custom_call" | custom-call | tf_op jit(solution)/shard_map/block_grads/pallas_call | solution.py:143
  84.7 34.0 %all_to_all.17 = bf16[16,128,512]{2,1,0:T(8,128)(2,1)S(1)} all-to-all(bf16[16,128,512]{2,1,0:T(8,128)(2,1)S(1)} %bitcast.5), channel_id=1, replica_groups={{1,3,5,7,9,11,13,15,17,19,21,23,25,27,29,31},{33,35,37,39,41,43,45,47,4..., dimensions={0} | all-to-all | bytes 4194304 | tf_op jit(solution)/shard_map/all_to_all | solution.py:44
  118.7 0.3 reduce_sum.12
  118.9 2.3 %collective-permute-start.4 = (bf16[128,512]{1,0:T(8,128)(2,1)S(1)}, bf16[128,512]{1,0:T(8,128)(2,1)S(1)}, u32[]{:S(2)}, u32[]{:S(2)}) collective-permute-start(bf16[128,512]{1,0:T(8,128)(2,1)S(1)} %reduce_sum.12), channel_id=1, source_target_pairs={{0,1},{1,0},{2,3},{3,2},{4,5},{5,4},{6,7},{7,6},{8,9},{9,8},{10,11... | collective-permute-start | bytes 393224 | tf_op jit(solution)/shard_map/ppermute | solution.py:40
  121.3 1.0 collective-permute-done.4
  122.2 0.7 slice_select_fusion
  (4 shorter events, 0.1 us)
Async XLA Ops:
  1.5 9.7 %collective-permute-start = (bf16[64,512]{1,0:T(8,128)(2,1)S(1)}, bf16[64,512]{1,0:T(8,128)(2,1)S(1)}, u32[]{:S(2)}, u32[]{:S(2)}) collective-permute-start(bf16[64,512]{1,0:T(8,128)(2,1)S(1)} %get-tuple-element.9), channel_id=1, source_target_pairs={{0,1},{1,0},{2,3},{3,2},{4,5},{5,4},{6,7},{7,6},{8,9},{9,8},{10,11... | collective-permute-start | bytes 196616 | tf_op jit(solution)/shard_map/ppermute | solution.py:40
  11.4 38.9 %copy-start = (s32[64]{0:T(128)S(1)}, s32[64]{0:T(128)}, u32[]{:S(2)}) copy-start(s32[64]{0:T(128)} %param.5) | copy-start | bytes 772
  42.1 12.2 %collective-permute-start.1 = (bf16[2048,512]{1,0:T(8,128)(2,1)}, bf16[2048,512]{1,0:T(8,128)(2,1)S(1)}, u32[]{:S(2)}, u32[]{:S(2)}) collective-permute-start(bf16[2048,512]{1,0:T(8,128)(2,1)} %bitcast.x_ref), channel_id=1, source_target_pairs={{0,1},{1,0},{2,3},{3,2},{4,5},{5,4},{6,7},{7,6},{8,9},{9,8},{10,11... | collective-permute-start | bytes 6291464 | tf_op jit(solution)/shard_map/ppermute | solution.py:40
  50.3 3.8 %collective-permute-start.2 = (s32[64]{0:T(128)S(1)}, s32[64]{0:T(128)S(1)}, u32[]{:S(2)}, u32[]{:S(2)}) collective-permute-start(s32[64]{0:T(128)S(1)} %copy-done), channel_id=1, source_target_pairs={{0,1},{1,0},{2,3},{3,2},{4,5},{5,4},{6,7},{7,6},{8,9},{9,8},{10,11... | collective-permute-start | bytes 776 | tf_op jit(solution)/shard_map/ppermute | solution.py:40
  76.4 3.1 %collective-permute-start.3 = (f32[32,128]{1,0:T(8,128)S(1)}, f32[32,128]{1,0:T(8,128)S(1)}, u32[]{:S(2)}, u32[]{:S(2)}) collective-permute-start(f32[32,128]{1,0:T(8,128)S(1)} %combine.1.own_ref), channel_id=1, source_target_pairs={{0,1},{1,0},{2,3},{3,2},{4,5},{5,4},{6,7},{7,6},{8,9},{9,8},{10,11... | collective-permute-start | bytes 49160 | tf_op jit(solution)/shard_map/ppermute | solution.py:40
  118.9 3.3 %collective-permute-start.4 = (bf16[128,512]{1,0:T(8,128)(2,1)S(1)}, bf16[128,512]{1,0:T(8,128)(2,1)S(1)}, u32[]{:S(2)}, u32[]{:S(2)}) collective-permute-start(bf16[128,512]{1,0:T(8,128)(2,1)S(1)} %reduce_sum.12), channel_id=1, source_target_pairs={{0,1},{1,0},{2,3},{3,2},{4,5},{5,4},{6,7},{7,6},{8,9},{9,8},{10,11... | collective-permute-start | bytes 393224 | tf_op jit(solution)/shard_map/ppermute | solution.py:40

commit v8 on v7

--- a/solution.py
+++ b/solution.py
@@ -120,8 +120,7 @@
     )
 
 
-def grads_kernel(s_ref, y_ref, own_ref, other_ref, out_ref):
-    block = out_ref.shape[0]
+def grads_kernel(block, s_ref, y_ref, own_ref, other_ref, out_ref):
     count = block // LANES
     step = pl.program_id(0)
     lx = columns(own_ref, step * count, count)
@@ -134,17 +133,17 @@
         w = jnp.where(kx == other_ref[G + r : G + r + 1, :], w - 1.0 / TAU, w)
         weights.append(w.astype(jnp.bfloat16))
     w = jnp.concatenate(weights, axis=1)
-    out_ref[...] = dot(w, y_ref[...], ((1,), (0,))).astype(jnp.bfloat16)
+    out_ref[rows, :] = dot(w, y_ref[...], ((1,), (0,))).astype(jnp.bfloat16)
 
 
 def block_grads(scores, y, own, other, block=1024):
     rows = scores.shape[0]
     width = y.shape[1]
     return pl.pallas_call(
-        grads_kernel,
+        functools.partial(grads_kernel, block),
         grid=(rows // block,),
         in_specs=[VMEM, VMEM, VMEM, VMEM],
-        out_specs=pl.BlockSpec((block, width), lambda i: (i, 0)),
+        out_specs=VMEM,
         out_shape=jax.ShapeDtypeStruct((rows, width), jnp.bfloat16),
         compiler_params=pltpu.CompilerParams(vmem_limit_bytes=28 << 20),
         name="block_grads",

time: 123 us -> 123 us (level)
  no operation moved by 1% of the time
where the time goes in v8:
time: 123 us
  blocking collectives  79 us (64%)
  starting transfers between devices  23.5 us (19%)
  Pallas kernels  12.8 us (10%)
  waiting for transfers between devices  4.61 us (4%)
  other arithmetic  1.95 us (2%)
    all_to_all x3, blocking collectives, exchange(): return lax.all_to_all(x, AX, 0, 0, axis_index_groups=GROUPS)  79 us
    ppermute x5, starting transfers between devices, swap(): return lax.ppermute(x, AX, CORES)  23.5 us
    pallas_call x1, Pallas kernels, block_stats(): pl.pallas_call(functools.partial(stats_kernel, chunks), grid=(steps,), in...  7.63 us
    pallas_call x1, Pallas kernels, block_grads(): pl.pallas_call(functools.partial(grads_kernel, block), grid=(rows // bloc...  5.16 us
    ppermute x5, waiting for transfers between devices, swap(): return lax.ppermute(x, AX, CORES)  4.61 us
  transfers between devices with their start and end apart: 5, of which 5 were waited for; matrix products, arithmetic and copies ran while one was open for 0% of the time, Pallas kernels for 0%

profile of v8, /device:TPU:1, one launch (start us, length us, event | category | flops | bytes accessed | tf_op | source)
XLA Modules:
  0.0 122.9 jit_solution(7227831028604604705)
XLA Ops:
  0.6 0.9 broadcast_select_fusion.1
  1.5 8.8 %collective-permute-start = (bf16[64,512]{1,0:T(8,128)(2,1)S(1)}, bf16[64,512]{1,0:T(8,128)(2,1)S(1)}, u32[]{:S(2)}, u32[]{:S(2)}) collective-permute-start(bf16[64,512]{1,0:T(8,128)(2,1)S(1)} %get-tuple-element.9), channel_id=1, source_target_pairs={{0,1},{1,0},{2,3},{3,2},{4,5},{5,4},{6,7},{7,6},{8,9},{9,8},{10,11... | collective-permute-start | bytes 196616 | tf_op jit(solution)/shard_map/ppermute | solution.py:40
  10.3 0.9 collective-permute-done
  11.2 0.2 broadcast_in_dim.4
  11.4 0.0 copy-start
  11.5 30.7 %all_to_all.15 = bf16[16,128,512]{2,1,0:T(8,128)(2,1)} all-to-all(bf16[16,128,512]{2,1,0:T(8,128)(2,1)S(1)} %broadcast_in_dim.4), channel_id=1, replica_groups={{1,3,5,7,9,11,13,15,17,19,21,23,25,27,29,31},{33,35,37,39,41,43,45,47,4..., dimensions={0} | all-to-all | bytes 4194304 | tf_op jit(solution)/shard_map/all_to_all | solution.py:44
  42.1 8.2 %collective-permute-start.1 = (bf16[2048,512]{1,0:T(8,128)(2,1)}, bf16[2048,512]{1,0:T(8,128)(2,1)S(1)}, u32[]{:S(2)}, u32[]{:S(2)}) collective-permute-start(bf16[2048,512]{1,0:T(8,128)(2,1)} %bitcast.x_ref), channel_id=1, source_target_pairs={{0,1},{1,0},{2,3},{3,2},{4,5},{5,4},{6,7},{7,6},{8,9},{9,8},{10,11... | collective-permute-start | bytes 6291464 | tf_op jit(solution)/shard_map/ppermute | solution.py:40
  50.3 0.0 copy-done
  50.3 1.9 %collective-permute-start.2 = (s32[64]{0:T(128)S(1)}, s32[64]{0:T(128)S(1)}, u32[]{:S(2)}, u32[]{:S(2)}) collective-permute-start(s32[64]{0:T(128)S(1)} %copy-done), channel_id=1, source_target_pairs={{0,1},{1,0},{2,3},{3,2},{4,5},{5,4},{6,7},{7,6},{8,9},{9,8},{10,11... | collective-permute-start | bytes 776 | tf_op jit(solution)/shard_map/ppermute | solution.py:40
  52.3 1.8 %collective-permute-done.2 = s32[64]{0:T(128)S(1)} collective-permute-done((s32[64]{0:T(128)S(1)}, s32[64]{0:T(128)S(1)}, u32[]{:S(2)}, u32[]{:S(2)}) %collective-permute-start.2) | collective-permute-done | bytes 288 | tf_op jit(solution)/shard_map/ppermute | solution.py:40
  54.1 0.1 fusion
  54.2 0.1 collective-permute-done.1.y_ref
  54.3 7.6 %block_stats.1 = (f32[4,4,128]{2,1,0:T(4,128)S(1)}, f32[2048,2048]{1,0:T(8,128)S(1)}) custom-call(bf16[2048,512]{1,0:T(8,128)(2,1)} %bitcast.x_ref, bf16[2048,512]{1,0:T(8,128)(2,1)S(1)} %collective-permute-done.1.y_ref), custom_call_target="tpu_custom_call" | custom-call | tf_op jit(solution)/shard_map/block_stats/pallas_call | solution.py:81
  62.0 14.4 %all_to_all.16.stats_ref = f32[16,17,128]{2,1,0:T(8,128)S(1)} all-to-all(f32[16,17,128]{2,1,0:T(8,128)S(1)} %broadcast_in_dim.5), channel_id=1, replica_groups={{1,3,5,7,9,11,13,15,17,19,21,23,25,27,29,31},{33,35,37,39,41,43,45,47,4..., dimensions={0} | all-to-all | bytes 278528 | tf_op jit(solution)/shard_map/all_to_all | solution.py:44
  76.4 2.3 %collective-permute-start.3 = (f32[32,128]{1,0:T(8,128)S(1)}, f32[32,128]{1,0:T(8,128)S(1)}, u32[]{:S(2)}, u32[]{:S(2)}) collective-permute-start(f32[32,128]{1,0:T(8,128)S(1)} %combine.1.own_ref), channel_id=1, source_target_pairs={{0,1},{1,0},{2,3},{3,2},{4,5},{5,4},{6,7},{7,6},{8,9},{9,8},{10,11... | collective-permute-start | bytes 49160 | tf_op jit(solution)/shard_map/ppermute | solution.py:40
  78.7 0.8 collective-permute-done.3.other_ref
  79.5 5.2 %block_grads.1 = bf16[2048,512]{1,0:T(8,128)(2,1)S(1)} custom-call(f32[2048,2048]{1,0:T(8,128)S(1)} %get-tuple-element.4.s_ref, bf16[2048,512]{1,0:T(8,128)(2,1)S(1)} %collective-permute-done.1.y_ref, f32[32,128]{1,0:T(8,128)S(1)} %combine.1.own_ref, f32[32,128]{1,0:T(8,128)S(1)} %collective-permute-done.3.other_ref), custom_call_target="tpu_custom_call" | custom-call | tf_op jit(solution)/shard_map/block_grads/pallas_call | solution.py:142
  84.7 34.0 %all_to_all.17 = bf16[16,128,512]{2,1,0:T(8,128)(2,1)S(1)} all-to-all(bf16[16,128,512]{2,1,0:T(8,128)(2,1)S(1)} %bitcast.5), channel_id=1, replica_groups={{1,3,5,7,9,11,13,15,17,19,21,23,25,27,29,31},{33,35,37,39,41,43,45,47,4..., dimensions={0} | all-to-all | bytes 4194304 | tf_op jit(solution)/shard_map/all_to_all | solution.py:44
  118.7 0.3 reduce_sum.12
  118.9 2.3 %collective-permute-start.4 = (bf16[128,512]{1,0:T(8,128)(2,1)S(1)}, bf16[128,512]{1,0:T(8,128)(2,1)S(1)}, u32[]{:S(2)}, u32[]{:S(2)}) collective-permute-start(bf16[128,512]{1,0:T(8,128)(2,1)S(1)} %reduce_sum.12), channel_id=1, source_target_pairs={{0,1},{1,0},{2,3},{3,2},{4,5},{5,4},{6,7},{7,6},{8,9},{9,8},{10,11... | collective-permute-start | bytes 393224 | tf_op jit(solution)/shard_map/ppermute | solution.py:40
  121.3 1.0 collective-permute-done.4
  122.2 0.7 slice_select_fusion
  (4 shorter events, 0.1 us)
Async XLA Ops:
  1.5 9.7 %collective-permute-start = (bf16[64,512]{1,0:T(8,128)(2,1)S(1)}, bf16[64,512]{1,0:T(8,128)(2,1)S(1)}, u32[]{:S(2)}, u32[]{:S(2)}) collective-permute-start(bf16[64,512]{1,0:T(8,128)(2,1)S(1)} %get-tuple-element.9), channel_id=1, source_target_pairs={{0,1},{1,0},{2,3},{3,2},{4,5},{5,4},{6,7},{7,6},{8,9},{9,8},{10,11... | collective-permute-start | bytes 196616 | tf_op jit(solution)/shard_map/ppermute | solution.py:40
  11.4 38.9 %copy-start = (s32[64]{0:T(128)S(1)}, s32[64]{0:T(128)}, u32[]{:S(2)}) copy-start(s32[64]{0:T(128)} %param.5) | copy-start | bytes 772
  42.1 12.2 %collective-permute-start.1 = (bf16[2048,512]{1,0:T(8,128)(2,1)}, bf16[2048,512]{1,0:T(8,128)(2,1)S(1)}, u32[]{:S(2)}, u32[]{:S(2)}) collective-permute-start(bf16[2048,512]{1,0:T(8,128)(2,1)} %bitcast.x_ref), channel_id=1, source_target_pairs={{0,1},{1,0},{2,3},{3,2},{4,5},{5,4},{6,7},{7,6},{8,9},{9,8},{10,11... | collective-permute-start | bytes 6291464 | tf_op jit(solution)/shard_map/ppermute | solution.py:40
  50.3 3.8 %collective-permute-start.2 = (s32[64]{0:T(128)S(1)}, s32[64]{0:T(128)S(1)}, u32[]{:S(2)}, u32[]{:S(2)}) collective-permute-start(s32[64]{0:T(128)S(1)} %copy-done), channel_id=1, source_target_pairs={{0,1},{1,0},{2,3},{3,2},{4,5},{5,4},{6,7},{7,6},{8,9},{9,8},{10,11... | collective-permute-start | bytes 776 | tf_op jit(solution)/shard_map/ppermute | solution.py:40
  76.4 3.1 %collective-permute-start.3 = (f32[32,128]{1,0:T(8,128)S(1)}, f32[32,128]{1,0:T(8,128)S(1)}, u32[]{:S(2)}, u32[]{:S(2)}) collective-permute-start(f32[32,128]{1,0:T(8,128)S(1)} %combine.1.own_ref), channel_id=1, source_target_pairs={{0,1},{1,0},{2,3},{3,2},{4,5},{5,4},{6,7},{7,6},{8,9},{9,8},{10,11... | collective-permute-start | bytes 49160 | tf_op jit(solution)/shard_map/ppermute | solution.py:40
  118.9 3.3 %collective-permute-start.4 = (bf16[128,512]{1,0:T(8,128)(2,1)S(1)}, bf16[128,512]{1,0:T(8,128)(2,1)S(1)}, u32[]{:S(2)}, u32[]{:S(2)}) collective-permute-start(bf16[128,512]{1,0:T(8,128)(2,1)S(1)} %reduce_sum.12), channel_id=1, source_target_pairs={{0,1},{1,0},{2,3},{3,2},{4,5},{5,4},{6,7},{7,6},{8,9},{9,8},{10,11... | collective-permute-start | bytes 393224 | tf_op jit(solution)/shard_map/ppermute | solution.py:40

commit v9 on v8

--- a/solution.py
+++ b/solution.py
@@ -167,9 +167,9 @@
     grad_part = block_grads(scores, y, own, swap(own))
     grads = exchange(grad_part.reshape(G, NC * n, width))
     grad = jnp.sum(grads.astype(jnp.float32), axis=0).astype(jnp.bfloat16)
-    grad_got = swap(grad)
-    motion_grad = jnp.where(is_text, grad_got[:n], grad[n:])
-    text_grad = jnp.where(is_text, grad[:n], grad_got[n:])
+    grad_got = swap(jnp.where(is_text, grad[n:], grad[:n]))
+    motion_grad = jnp.where(is_text, grad_got, grad[n:])
+    text_grad = jnp.where(is_text, grad[:n], grad_got)
     return (motion_grad, text_grad)
 
 

time: 123 us -> 123 us (level)
  no operation moved by 1% of the time
where the time goes in v9:
time: 123 us
  blocking collectives  79 us (64%)
  starting transfers between devices  23.5 us (19%)
  Pallas kernels  12.8 us (10%)
  waiting for transfers between devices  4.52 us (4%)
  other arithmetic  1.96 us (2%)
    all_to_all x3, blocking collectives, exchange(): return lax.all_to_all(x, AX, 0, 0, axis_index_groups=GROUPS)  79 us
    ppermute x5, starting transfers between devices, swap(): return lax.ppermute(x, AX, CORES)  23.5 us
    pallas_call x1, Pallas kernels, block_stats(): pl.pallas_call(functools.partial(stats_kernel, chunks), grid=(steps,), in...  7.63 us
    pallas_call x1, Pallas kernels, block_grads(): pl.pallas_call(functools.partial(grads_kernel, block), grid=(rows // bloc...  5.16 us
    ppermute x5, waiting for transfers between devices, swap(): return lax.ppermute(x, AX, CORES)  4.52 us
  transfers between devices with their start and end apart: 5, of which 5 were waited for; matrix products, arithmetic and copies ran while one was open for 0% of the time, Pallas kernels for 0%

profile of v9, /device:TPU:1, one launch (start us, length us, event | category | flops | bytes accessed | tf_op | source)
XLA Modules:
  0.0 122.8 jit_solution(4017716837374591795)
XLA Ops:
  0.6 0.9 broadcast_select_fusion.4
  1.5 8.8 %collective-permute-start = (bf16[64,512]{1,0:T(8,128)(2,1)S(1)}, bf16[64,512]{1,0:T(8,128)(2,1)S(1)}, u32[]{:S(2)}, u32[]{:S(2)}) collective-permute-start(bf16[64,512]{1,0:T(8,128)(2,1)S(1)} %get-tuple-element.9), channel_id=1, source_target_pairs={{0,1},{1,0},{2,3},{3,2},{4,5},{5,4},{6,7},{7,6},{8,9},{9,8},{10,11... | collective-permute-start | bytes 196616 | tf_op jit(solution)/shard_map/ppermute | solution.py:40
  10.3 0.9 collective-permute-done
  11.2 0.2 broadcast_in_dim.4
  11.4 0.0 copy-start
  11.5 30.7 %all_to_all.15 = bf16[16,128,512]{2,1,0:T(8,128)(2,1)} all-to-all(bf16[16,128,512]{2,1,0:T(8,128)(2,1)S(1)} %broadcast_in_dim.4), channel_id=1, replica_groups={{1,3,5,7,9,11,13,15,17,19,21,23,25,27,29,31},{33,35,37,39,41,43,45,47,4..., dimensions={0} | all-to-all | bytes 4194304 | tf_op jit(solution)/shard_map/all_to_all | solution.py:44
  42.1 8.2 %collective-permute-start.1 = (bf16[2048,512]{1,0:T(8,128)(2,1)}, bf16[2048,512]{1,0:T(8,128)(2,1)S(1)}, u32[]{:S(2)}, u32[]{:S(2)}) collective-permute-start(bf16[2048,512]{1,0:T(8,128)(2,1)} %bitcast.x_ref), channel_id=1, source_target_pairs={{0,1},{1,0},{2,3},{3,2},{4,5},{5,4},{6,7},{7,6},{8,9},{9,8},{10,11... | collective-permute-start | bytes 6291464 | tf_op jit(solution)/shard_map/ppermute | solution.py:40
  50.3 0.0 copy-done
  50.3 1.9 %collective-permute-start.2 = (s32[64]{0:T(128)S(1)}, s32[64]{0:T(128)S(1)}, u32[]{:S(2)}, u32[]{:S(2)}) collective-permute-start(s32[64]{0:T(128)S(1)} %copy-done), channel_id=1, source_target_pairs={{0,1},{1,0},{2,3},{3,2},{4,5},{5,4},{6,7},{7,6},{8,9},{9,8},{10,11... | collective-permute-start | bytes 776 | tf_op jit(solution)/shard_map/ppermute | solution.py:40
  52.3 1.8 %collective-permute-done.2 = s32[64]{0:T(128)S(1)} collective-permute-done((s32[64]{0:T(128)S(1)}, s32[64]{0:T(128)S(1)}, u32[]{:S(2)}, u32[]{:S(2)}) %collective-permute-start.2) | collective-permute-done | bytes 288 | tf_op jit(solution)/shard_map/ppermute | solution.py:40
  54.1 0.1 fusion
  54.2 0.1 collective-permute-done.1.y_ref
  54.3 7.6 %block_stats.1 = (f32[4,4,128]{2,1,0:T(4,128)S(1)}, f32[2048,2048]{1,0:T(8,128)S(1)}) custom-call(bf16[2048,512]{1,0:T(8,128)(2,1)} %bitcast.x_ref, bf16[2048,512]{1,0:T(8,128)(2,1)S(1)} %collective-permute-done.1.y_ref), custom_call_target="tpu_custom_call" | custom-call | tf_op jit(solution)/shard_map/block_stats/pallas_call | solution.py:81
  62.0 14.4 %all_to_all.16.stats_ref = f32[16,17,128]{2,1,0:T(8,128)S(1)} all-to-all(f32[16,17,128]{2,1,0:T(8,128)S(1)} %broadcast_in_dim.5), channel_id=1, replica_groups={{1,3,5,7,9,11,13,15,17,19,21,23,25,27,29,31},{33,35,37,39,41,43,45,47,4..., dimensions={0} | all-to-all | bytes 278528 | tf_op jit(solution)/shard_map/all_to_all | solution.py:44
  76.4 2.3 %collective-permute-start.3 = (f32[32,128]{1,0:T(8,128)S(1)}, f32[32,128]{1,0:T(8,128)S(1)}, u32[]{:S(2)}, u32[]{:S(2)}) collective-permute-start(f32[32,128]{1,0:T(8,128)S(1)} %combine.1.own_ref), channel_id=1, source_target_pairs={{0,1},{1,0},{2,3},{3,2},{4,5},{5,4},{6,7},{7,6},{8,9},{9,8},{10,11... | collective-permute-start | bytes 49160 | tf_op jit(solution)/shard_map/ppermute | solution.py:40
  78.7 0.8 collective-permute-done.3.other_ref
  79.5 5.2 %block_grads.1 = bf16[2048,512]{1,0:T(8,128)(2,1)S(1)} custom-call(f32[2048,2048]{1,0:T(8,128)S(1)} %get-tuple-element.4.s_ref, bf16[2048,512]{1,0:T(8,128)(2,1)S(1)} %collective-permute-done.1.y_ref, f32[32,128]{1,0:T(8,128)S(1)} %combine.1.own_ref, f32[32,128]{1,0:T(8,128)S(1)} %collective-permute-done.3.other_ref), custom_call_target="tpu_custom_call" | custom-call | tf_op jit(solution)/shard_map/block_grads/pallas_call | solution.py:142
  84.7 34.0 %all_to_all.17 = bf16[16,128,512]{2,1,0:T(8,128)(2,1)S(1)} all-to-all(bf16[16,128,512]{2,1,0:T(8,128)(2,1)S(1)} %bitcast.5), channel_id=1, replica_groups={{1,3,5,7,9,11,13,15,17,19,21,23,25,27,29,31},{33,35,37,39,41,43,45,47,4..., dimensions={0} | all-to-all | bytes 4194304 | tf_op jit(solution)/shard_map/all_to_all | solution.py:44
  118.7 0.3 reduce_sum.12
  119.0 2.3 %collective-permute-start.4 = (bf16[64,512]{1,0:T(8,128)(2,1)S(1)}, bf16[64,512]{1,0:T(8,128)(2,1)S(1)}, u32[]{:S(2)}, u32[]{:S(2)}) collective-permute-start(bf16[64,512]{1,0:T(8,128)(2,1)S(1)} %broadcast_select_fusion.2), channel_id=1, source_target_pairs={{0,1},{1,0},{2,3},{3,2},{4,5},{5,4},{6,7},{7,6},{8,9},{9,8},{10,11... | collective-permute-start | bytes 196616 | tf_op jit(solution)/shard_map/ppermute | solution.py:40
  121.3 0.9 collective-permute-done.4
  122.2 0.7 broadcast_select_fusion
  (5 shorter events, 0.1 us)
Async XLA Ops:
  1.5 9.7 %collective-permute-start = (bf16[64,512]{1,0:T(8,128)(2,1)S(1)}, bf16[64,512]{1,0:T(8,128)(2,1)S(1)}, u32[]{:S(2)}, u32[]{:S(2)}) collective-permute-start(bf16[64,512]{1,0:T(8,128)(2,1)S(1)} %get-tuple-element.9), channel_id=1, source_target_pairs={{0,1},{1,0},{2,3},{3,2},{4,5},{5,4},{6,7},{7,6},{8,9},{9,8},{10,11... | collective-permute-start | bytes 196616 | tf_op jit(solution)/shard_map/ppermute | solution.py:40
  11.4 38.9 %copy-start = (s32[64]{0:T(128)S(1)}, s32[64]{0:T(128)}, u32[]{:S(2)}) copy-start(s32[64]{0:T(128)} %param.5) | copy-start | bytes 772
  42.1 12.2 %collective-permute-start.1 = (bf16[2048,512]{1,0:T(8,128)(2,1)}, bf16[2048,512]{1,0:T(8,128)(2,1)S(1)}, u32[]{:S(2)}, u32[]{:S(2)}) collective-permute-start(bf16[2048,512]{1,0:T(8,128)(2,1)} %bitcast.x_ref), channel_id=1, source_target_pairs={{0,1},{1,0},{2,3},{3,2},{4,5},{5,4},{6,7},{7,6},{8,9},{9,8},{10,11... | collective-permute-start | bytes 6291464 | tf_op jit(solution)/shard_map/ppermute | solution.py:40
  50.3 3.8 %collective-permute-start.2 = (s32[64]{0:T(128)S(1)}, s32[64]{0:T(128)S(1)}, u32[]{:S(2)}, u32[]{:S(2)}) collective-permute-start(s32[64]{0:T(128)S(1)} %copy-done), channel_id=1, source_target_pairs={{0,1},{1,0},{2,3},{3,2},{4,5},{5,4},{6,7},{7,6},{8,9},{9,8},{10,11... | collective-permute-start | bytes 776 | tf_op jit(solution)/shard_map/ppermute | solution.py:40
  76.4 3.1 %collective-permute-start.3 = (f32[32,128]{1,0:T(8,128)S(1)}, f32[32,128]{1,0:T(8,128)S(1)}, u32[]{:S(2)}, u32[]{:S(2)}) collective-permute-start(f32[32,128]{1,0:T(8,128)S(1)} %combine.1.own_ref), channel_id=1, source_target_pairs={{0,1},{1,0},{2,3},{3,2},{4,5},{5,4},{6,7},{7,6},{8,9},{9,8},{10,11... | collective-permute-start | bytes 49160 | tf_op jit(solution)/shard_map/ppermute | solution.py:40
  119.0 3.2 %collective-permute-start.4 = (bf16[64,512]{1,0:T(8,128)(2,1)S(1)}, bf16[64,512]{1,0:T(8,128)(2,1)S(1)}, u32[]{:S(2)}, u32[]{:S(2)}) collective-permute-start(bf16[64,512]{1,0:T(8,128)(2,1)S(1)} %broadcast_select_fusion.2), channel_id=1, source_target_pairs={{0,1},{1,0},{2,3},{3,2},{4,5},{5,4},{6,7},{7,6},{8,9},{9,8},{10,11... | collective-permute-start | bytes 196616 | tf_op jit(solution)/shard_map/ppermute | solution.py:40
